TPU v7x, 128 devices: a whole 4x4x4 slice. The times are simulated.
128 devices in a mesh: sweep: 32 (over z, x, core), grp: 4 (over y).
Axes of the slice: x: 4, y: 4, z: 4, core: 2. Of those that a mesh axis runs over, the one named last changes fastest.
Arguments:
- state: float32 [4, 128, 6, 4096], P('grp', 'sweep'), may hold values from -6 to 6
- forcing: float32 [4, 128, 6, 4096], P('grp', 'sweep'), may hold values from -6 to 6
- viscosity: float32 [4, 128, 4096], P('grp', 'sweep'), may hold values from 0.05 to 0.5
- inverses: float32 [4, 128, 6, 6], P('grp', 'sweep'), as said below
- lower_jac: float32 [4, 128, 6, 6], P('grp', 'sweep')
- upper_jac: float32 [4, 128, 6, 6], P('grp', 'sweep')
- diag_scale: float32 [4, 128, 4096], P('grp', 'sweep'), may hold values from 0.99 to 1
- lower_coupling: float32 [4, 128, 4096], P('grp', 'sweep'), may hold values from 0.3 to 1
- upper_coupling: float32 [4, 128, 4096], P('grp', 'sweep'), may hold values from 0.3 to 1
- donor_block: int32 [128, 128, 32], P(('sweep', 'grp')), may hold values from 0 to 3
- donor_point: int32 [128, 128, 32], P(('sweep', 'grp')), may hold values from 0 to 4092
- donor_weight: float32 [128, 128, 32, 4], P(('sweep', 'grp')), may hold values from 0.1 to 1
- fringe_block: int32 [128, 128, 32], P(('sweep', 'grp')), may hold values from 0 to 3
- fringe_point: int32 [128, 128, 32], P(('sweep', 'grp')), may hold values from 0 to 4095
- block_order: int32 [4, 128], P('grp', 'sweep'), may hold values from 0 to 3, as said below
Outputs:
- new_state: float32 [4, 128, 6, 4096], P('grp', 'sweep')
- correction: float32 [4, 128, 6, 4096], P('grp', 'sweep')
Inputs may be any that keep to these rules, and one draw needn't show every extreme that they name: `block_order`: each device's 4 consecutive entries of a lane are a permutation of 0 to 3. `inverses`: diagonally dominant.
All inputs are finite; a program needn't handle non-finite values.
Results may differ from a plain program's by a relative error of at most 0.0003.
Values sent between devices are 32-bit elements; how exact they have to be, the bound alone decides.
No kernel may reach another device: no remote copies, remote signals or barrier semaphores. Data moves between devices by JAX's collectives and lax.ppermute only.
A program may use at most 64 MiB of HBM per device.

v0:
```python
import math

import jax
import jax.numpy as jnp
from jax import lax
from jax.sharding import PartitionSpec as P

STEPS = 2


def from_behind(value, axis, steps):
    count = lax.axis_size(axis)
    first, last = (max(0, -steps), min(count, count - steps))
    return lax.ppermute(value, axis, [(source, source + steps) for source in range(first, last)])


def apply_gmat(gmat, field):
    return jnp.einsum("ij,jp->ip", gmat, field, precision=lax.Precision.HIGHEST)


def combine_maps(earlier, later):
    first_f, first_m, first_v = earlier
    second_f, second_m, second_v = later
    merged_m = jnp.einsum("ij,jk->ik", second_m, first_m, precision=lax.Precision.HIGHEST)
    return (second_f * first_f, merged_m, second_f * apply_gmat(second_m, first_v) + second_v)


def compose_local(gmats, factor, offset, visit):
    points = offset.shape[2]
    width = offset.shape[1]
    total_f = jnp.ones((points,), jnp.float32)
    total_m = jnp.eye(width, dtype=jnp.float32)
    total_v = jnp.zeros((width, points), jnp.float32)
    for index in visit:
        total_f, total_m, total_v = combine_maps(
            (total_f, total_m, total_v), (factor[index], gmats[index], offset[index])
        )
    return (total_f, total_m, total_v)


def apply_local(gmats, factor, offset, incoming, visit):
    carry = incoming
    outputs = [None] * offset.shape[0]
    for index in visit:
        carry = factor[index][None, :] * apply_gmat(gmats[index], carry) + offset[index]
        outputs[index] = carry
    return jnp.stack(outputs)


def to_tiles(fields):
    blocks, width, points = fields.shape
    return (
        fields.reshape(blocks, width, points // 128, 128)
        .transpose(0, 2, 1, 3)
        .reshape(blocks * (points // 128), width, 128)
    )


def from_tiles(tiles, blocks, points):
    width = tiles.shape[1]
    return (
        tiles.reshape(blocks, points // 128, width, 128)
        .transpose(0, 2, 1, 3)
        .reshape(blocks, width, points)
    )


def interpolate(tiles, per_block, blk_flat, pt_flat, weight_flat):
    count, width, _ = tiles.shape
    total = blk_flat.shape[0]
    group = math.gcd(total, 512)
    stencil = weight_flat.shape[1]
    lanes = jnp.arange(256, dtype=jnp.int32)

    def interpolate_one_group(items):
        blk, point, weights = items
        first = blk * per_block + point // 128
        second = jnp.minimum(first + 1, count - 1)
        window = jnp.concatenate([tiles[first], tiles[second]], axis=2)
        offset = point % 128
        weight_row = jnp.zeros((blk.shape[0], 256), jnp.float32)
        for j in range(stencil):
            weight_row = weight_row + jnp.where(
                lanes[None, :] == (offset + j)[:, None], weights[:, j : j + 1], 0.0
            )
        return jnp.sum(window * weight_row[:, None, :], axis=2)

    grouped = (
        blk_flat.reshape(-1, group),
        pt_flat.reshape(-1, group),
        weight_flat.reshape(-1, group, stencil),
    )
    return lax.map(interpolate_one_group, grouped).reshape(total, width)


def fringe_terms(tiles, per_block, blk_flat, pt_flat, got_flat):
    count, width, _ = tiles.shape
    total = blk_flat.shape[0]
    group = math.gcd(total, 512)
    lanes = jnp.arange(128, dtype=jnp.int32)
    tile_ids = jnp.arange(count, dtype=jnp.int32)

    def fringe_one_group(acc, items):
        blk, point, got = items
        index = blk * per_block + point // 128
        lane_hot = (lanes[None, :] == (point % 128)[:, None]).astype(jnp.float32)
        current = jnp.sum(tiles[index] * lane_hot[:, None, :], axis=2)
        delta = got - current
        spread = (delta[:, :, None] * lane_hot[:, None, :]).reshape(blk.shape[0], width * 128)
        tile_hot = (tile_ids[None, :] == index[:, None]).astype(jnp.float32)
        acc = acc + jnp.einsum("rt,rk->tk", tile_hot, spread, precision=lax.Precision.HIGHEST)
        return (acc, None)

    grouped = (
        blk_flat.reshape(-1, group),
        pt_flat.reshape(-1, group),
        got_flat.reshape(-1, group, width),
    )
    start = jnp.zeros((count, width * 128), jnp.float32)
    acc, _ = lax.scan(fringe_one_group, start, grouped)
    return acc.reshape(count, width, 128)


def per_device(
    state,
    forcing,
    viscosity,
    inverses,
    lower_jac,
    upper_jac,
    diag_scale,
    lower_coupling,
    upper_coupling,
    donor_block,
    donor_point,
    donor_weight,
    fringe_block,
    fringe_point,
    block_order,
):
    hi = lax.Precision.HIGHEST
    fields = state[0]
    blocks, width, points = fields.shape
    per_block = points // 128
    n_sweep = lax.axis_size("sweep")
    order = block_order[0]
    permute = (order[:, None] == jnp.arange(blocks, dtype=jnp.int32)[None, :]).astype(jnp.float32)
    g_low = jnp.einsum(
        "kb,bij->kij",
        permute,
        jnp.einsum("bij,bjk->bik", inverses[0], lower_jac[0], precision=hi),
        precision=hi,
    )
    g_up = jnp.einsum(
        "kb,bij->kij",
        permute,
        jnp.einsum("bij,bjk->bik", inverses[0], upper_jac[0], precision=hi),
        precision=hi,
    )
    low_factor = jnp.einsum("kb,bp->kp", permute, diag_scale[0] * lower_coupling[0], precision=hi)
    up_factor = jnp.einsum("kb,bp->kp", permute, upper_coupling[0], precision=hi)
    forward = list(range(blocks))
    backward = forward[::-1]
    stencil = donor_weight.shape[3]
    src_blk = donor_block[0].reshape(-1)
    src_pt = donor_point[0].reshape(-1)
    src_weight = donor_weight[0].reshape(-1, stencil)
    dst_blk = fringe_block[0].reshape(-1)
    dst_pt = fringe_point[0].reshape(-1)
    correction = jnp.zeros_like(fields)
    for step in range(STEPS):
        tiles = to_tiles(fields)
        interp = interpolate(tiles, per_block, src_blk, src_pt, src_weight).reshape(
            donor_point.shape[1], donor_point.shape[2], width
        )
        received = lax.all_to_all(interp, ("sweep", "grp"), split_axis=0, concat_axis=0, tiled=True)
        padded = jnp.pad(fields, ((0, 0), (0, 0), (1, 1)))
        residual = forcing[0] + viscosity[0][:, None, :] * (
            padded[..., 2:] - 2.0 * fields + padded[..., :-2]
        )
        added = fringe_terms(tiles, per_block, dst_blk, dst_pt, received.reshape(-1, width))
        residual = residual + from_tiles(added, blocks, points)
        solved = diag_scale[0][:, None, :] * jnp.einsum(
            "bij,bjp->bip", inverses[0], residual, precision=hi
        )
        solved_p = jnp.einsum("kb,bvp->kvp", permute, solved, precision=hi)
        low_map = compose_local(g_low, low_factor, solved_p, forward)

        def relay_low(turn, carried):
            arrived = from_behind(carried[1], "sweep", 1)
            leaving = low_map[0][None, :] * apply_gmat(low_map[1], arrived) + low_map[2]
            return (arrived, leaving)

        entering = lax.fori_loop(0, n_sweep, relay_low, (jnp.zeros_like(low_map[2]), low_map[2]))[0]
        star = apply_local(g_low, low_factor, solved_p, entering, forward)
        up_map = compose_local(g_up, up_factor, star, backward)

        def relay_up(turn, carried):
            arrived = from_behind(carried[1], "sweep", -1)
            leaving = up_map[0][None, :] * apply_gmat(up_map[1], arrived) + up_map[2]
            return (arrived, leaving)

        entering_up = lax.fori_loop(0, n_sweep, relay_up, (jnp.zeros_like(up_map[2]), up_map[2]))[0]
        corr_p = apply_local(g_up, up_factor, star, entering_up, backward)
        correction = jnp.einsum("kb,kvp->bvp", permute, corr_p, precision=hi)
        fields = fields + correction
    return (fields[None], correction[None])


def solution(mesh):
    return jax.shard_map(
        per_device,
        mesh=mesh,
        in_specs=(
            P("grp", "sweep", None, None),
            P("grp", "sweep", None, None),
            P("grp", "sweep", None),
            P("grp", "sweep", None, None),
            P("grp", "sweep", None, None),
            P("grp", "sweep", None, None),
            P("grp", "sweep", None),
            P("grp", "sweep", None),
            P("grp", "sweep", None),
            P(("sweep", "grp"), None, None),
            P(("sweep", "grp"), None, None),
            P(("sweep", "grp"), None, None, None),
            P(("sweep", "grp"), None, None),
            P(("sweep", "grp"), None, None),
            P("grp", "sweep"),
        ),
        out_specs=(P("grp", "sweep", None, None), P("grp", "sweep", None, None)),
        check_vma=False,
    )
```

profile of v0, /device:TPU:7, one launch (start us, length us, event | category | flops | bytes accessed | tf_op | source)
XLA Modules:
  0.0 1573.2 jit_solution(5789899548926020673)
XLA Ops:
  6.2 92.3 %while.110 = (s32[]{:T(128)}, f32[8,512,6]{1,0,2:T(8,128)}, s32[8,512]{1,0:T(8,128)}, s32[8,512]{1,0:T(8,128)}, f32[128,6,128]{2,1,0:T(8,128)S(1)}, /*index=5*/f32[8,512,4]{1,2,0:T(4,128)}, s32[]{:T(128)}, s32[]{:T(128)}) while((s32[]{:T(128)}, f32[8,512,6]{1,0,2:T(8,128)}, s32[8,512]{1,0:T(8,128)}, ...), condition=%wide.region_2.3_spmd.clone.clone, body=%wide.region_0.2_spmd.clone.clone.sunk | while | flops 3820034 | bytes 10666085 | solution.py:93
  100.8 10.8 all-to-all-start
  122.4 86.0 %while.112 = (s32[]{:T(128)}, f32[128,768]{1,0:T(8,128)}, s32[8,512]{1,0:T(8,128)}, s32[8,512]{1,0:T(8,128)}, f32[8,512,6]{1,0,2:T(8,128)}, /*index=5*/f32[128,6,128]{2,1,0:T(8,128)S(1)}, s32[]{:T(128)}, s32[]{:T(128)}) while((s32[]{:T(128)}, f32[128,768]{1,0:T(8,128)}, s32[8,512]{1,0:T(8,128)}, s32[8,512]{1,0:T(8,128)}, ...), condition=%wide.region_5.6_spmd.clone.clone, body=%wide.region_3.5_spmd.clone.clone.sunk | while | flops 605639680 | bytes 15878331 | solution.py:120
  213.9 287.1 %while.106 = (s32[]{:T(128)}, f32[6,4096]{1,0:T(8,128)}, f32[6,4096]{1,0:T(8,128)S(1)}, f32[4096]{0:T(1024)S(1)}, f32[6,6]{1,0:T(8,128)S(1)}, /*index=5*/f32[6,4096]{1,0:T(8,128)S(1)}, s32[]{:T(128)}) while((s32[]{:T(128)}, f32[6,4096]{1,0:T(8,128)}, f32[6,4096]{1,0:T(8,128)S(1)}, f32[4096]{0:T(1024)S(1)}, f32[6,6]{1,0:T(8,128)S(1)}, ...), condition=%wide.region_7.8_spmd, body=%wide.region_6.7_spmd.sunk | while | flops 1818626 | bytes 1098017 | solution.py:194
  504.5 290.0 %while.107 = (s32[]{:T(128)}, f32[6,4096]{1,0:T(8,128)}, f32[6,4096]{1,0:T(8,128)S(1)}, f32[4096]{0:T(1024)S(1)}, f32[6,6]{1,0:T(8,128)S(1)}, /*index=5*/f32[6,4096]{1,0:T(8,128)S(1)}, s32[]{:T(128)}) while((s32[]{:T(128)}, f32[6,4096]{1,0:T(8,128)}, f32[6,4096]{1,0:T(8,128)S(1)}, f32[4096]{0:T(1024)S(1)}, f32[6,6]{1,0:T(8,128)S(1)}, ...), condition=%wide.region_9.10_spmd, body=%wide.region_8.9_spmd.sunk | while | flops 1818626 | bytes 1098017 | solution.py:203
  506.4 7.2 collective-permute-done.1
  516.2 6.5 collective-permute-done.1
  525.2 6.5 collective-permute-done.1
  543.3 6.5 collective-permute-done.1
  552.4 6.5 collective-permute-done.1
  570.4 6.5 collective-permute-done.1
  579.5 6.5 collective-permute-done.1
  597.6 6.5 collective-permute-done.1
  606.6 6.5 collective-permute-done.1
  615.6 6.5 collective-permute-done.1
  624.7 6.5 collective-permute-done.1
  633.7 6.5 collective-permute-done.1
  642.8 6.5 collective-permute-done.1
  660.8 6.5 collective-permute-done.1
  669.9 6.5 collective-permute-done.1
  688.0 6.5 collective-permute-done.1
  697.0 6.5 collective-permute-done.1
  715.1 6.5 collective-permute-done.1
  724.1 6.5 collective-permute-done.1
  742.2 6.5 collective-permute-done.1
  751.3 6.5 collective-permute-done.1
  798.9 92.3 %while.111 = (s32[]{:T(128)}, f32[8,512,6]{1,0,2:T(8,128)}, s32[8,512]{1,0:T(8,128)}, s32[8,512]{1,0:T(8,128)}, f32[128,6,128]{2,1,0:T(8,128)S(1)}, /*index=5*/f32[8,512,4]{1,2,0:T(4,128)}, s32[]{:T(128)}, s32[]{:T(128)}) while((s32[]{:T(128)}, f32[8,512,6]{1,0,2:T(8,128)}, s32[8,512]{1,0:T(8,128)}, ...), condition=%wide.region_12.13_spmd.clone.clone, body=%wide.region_10.12_spmd.clone.clone.sunk | while | flops 3820034 | bytes 10666085 | solution.py:93
  899.6 8.3 all-to-all-done.1
  909.2 74.1 %while.113 = (s32[]{:T(128)}, f32[128,768]{1,0:T(8,128)}, s32[8,512]{1,0:T(8,128)}, s32[8,512]{1,0:T(8,128)}, f32[8,512,6]{1,0,2:T(8,128)S(1)}, /*index=5*/f32[128,6,128]{2,1,0:T(8,128)S(1)}, s32[]{:T(128)}, s32[]{:T(128)}) while((s32[]{:T(128)}, f32[128,768]{1,0:T(8,128)}, s32[8,512]{1,0:T(8,128)}, ...), condition=%wide.region_15.16_spmd.clone.clone, body=%wide.region_13.15_spmd.clone.clone.sunk | while | flops 605639680 | bytes 15870111 | solution.py:120
  988.9 287.1 %while.108 = (s32[]{:T(128)}, f32[6,4096]{1,0:T(8,128)}, f32[6,4096]{1,0:T(8,128)S(1)}, f32[4096]{0:T(1024)S(1)}, f32[6,6]{1,0:T(8,128)S(1)}, /*index=5*/f32[6,4096]{1,0:T(8,128)S(1)}, s32[]{:T(128)}) while((s32[]{:T(128)}, f32[6,4096]{1,0:T(8,128)}, f32[6,4096]{1,0:T(8,128)S(1)}, f32[4096]{0:T(1024)S(1)}, f32[6,6]{1,0:T(8,128)S(1)}, ...), condition=%wide.region_17.18_spmd, body=%wide.region_16.17_spmd.sunk | while | flops 1818626 | bytes 1098017 | solution.py:194
  1279.5 290.0 %while.109 = (s32[]{:T(128)}, f32[6,4096]{1,0:T(8,128)}, f32[6,4096]{1,0:T(8,128)S(1)}, f32[4096]{0:T(1024)S(1)}, f32[6,6]{1,0:T(8,128)S(1)}, /*index=5*/f32[6,4096]{1,0:T(8,128)S(1)}, s32[]{:T(128)}) while((s32[]{:T(128)}, f32[6,4096]{1,0:T(8,128)}, f32[6,4096]{1,0:T(8,128)S(1)}, f32[4096]{0:T(1024)S(1)}, f32[6,6]{1,0:T(8,128)S(1)}, ...), condition=%wide.region_19.20_spmd, body=%wide.region_18.19_spmd.sunk | while | flops 1818626 | bytes 1098017 | solution.py:203
  1281.5 7.2 collective-permute-done.3
  (1395 shorter events, 1403.8 us)
Async XLA Ops:
  100.8 19.1 %all-to-all-start = ((f32[128,1,192]{2,1,0:T(1,128)}), f32[128,1,192]{2,1,0:T(1,128)S(1)}, u32[]{:S(2)}, u32[]{:S(2)}) async-start(f32[128,1,192]{2,1,0:T(1,128)} %reshape.1166), calls=%async_computation | async-start | bytes 262144 | tf_op jit(solution)/shard_map/all_to_all | solution.py:176
  220.7 8.4 collective-permute-start
  229.8 8.4 collective-permute-start
  238.8 8.4 collective-permute-start
  247.8 8.4 collective-permute-start
  256.9 8.4 collective-permute-start
  265.9 8.4 collective-permute-start
  275.0 8.4 collective-permute-start
  284.0 8.4 collective-permute-start
  302.1 8.4 collective-permute-start
  311.1 8.4 collective-permute-start
  329.2 8.4 collective-permute-start
  338.3 8.4 collective-permute-start
  356.3 8.4 collective-permute-start
  365.4 8.4 collective-permute-start
  374.4 8.4 collective-permute-start
  383.5 8.4 collective-permute-start
  392.5 8.4 collective-permute-start
  401.5 8.4 collective-permute-start
  410.6 8.4 collective-permute-start
  419.6 8.4 collective-permute-start
  428.7 8.4 collective-permute-start
  437.7 8.4 collective-permute-start
  446.7 8.4 collective-permute-start
  455.8 8.4 collective-permute-start
  473.9 8.4 collective-permute-start
  482.9 8.4 collective-permute-start
  504.5 9.1 collective-permute-start.1
  893.4 14.5 all-to-all-start.1
  995.8 8.4 collective-permute-start.2
  1004.8 8.4 collective-permute-start.2
  1279.5 9.1 collective-permute-start.3
  (334 other events, 7201.4 us)
where the time goes:
time: 1590 us; the launch traced here: 1570 us
  waiting for transfers between devices  549 us (35%)
  starting transfers between devices  548 us (34%)
  local copies, waits for them, and re-layouts  274 us (17%)
  other arithmetic  103 us (6%)
  matrix products  93.3 us (6%)
    ppermute x128, waiting for transfers between devices, from_behind(): lax.ppermute(value, axis, [(source, source + steps) for source in range(f...  539 us
    ppermute x128, starting transfers between devices, from_behind(): lax.ppermute(value, axis, [(source, source + steps) for source in range(f...  531 us
    gather x32, local copies, waits for them, and re-layouts, interpolate_one_group(): window = jnp.concatenate([tiles[first], tiles[second]], axis=2)  73.3 us
    while x336, local copies, waits for them, and re-layouts  62 us
    dot_general x158, matrix products, apply_gmat(): return jnp.einsum('ij,jp->ip', gmat, field, precision=lax.Precision.HIGHEST)  44.8 us
    dot_general x16, matrix products, fringe_one_group(): jnp.einsum('rt,rk->tk', tile_hot, spread, precision=lax.Precision.HIGHEST)  41.1 us
    reduce_sum x16, other arithmetic, interpolate_one_group(): return jnp.sum(window * weight_row[:, None, :], axis=2)  37.6 us
  transfers between devices with their start and end apart: 130, of which 130 were waited for; matrix products, arithmetic and copies ran while one was open for 0% of the time, Pallas kernels for 0%

commit v1 on v0

v1 whole, which is shorter than its diff:
```python
import jax
import jax.numpy as jnp
from jax import lax
from jax.experimental import pallas as pl
from jax.experimental.pallas import tpu as pltpu
from jax.sharding import PartitionSpec as P

F32 = jnp.float32
BF16 = jnp.bfloat16
VARS = 6
BLK = 4
TILES = 32
SLOTS = 32
LANES = 128
HALF = 64
TAIL = 8
GROUP = 4
VMEM = pl.BlockSpec(memory_space=pltpu.VMEM)
SMEM = pl.BlockSpec(memory_space=pltpu.SMEM)
PARAMS = pltpu.CompilerParams(vmem_limit_bytes=40 * 1024 * 1024)


def to_rows(x):
    return x.reshape(BLK, VARS, TILES, LANES).transpose(1, 2, 0, 3).reshape(VARS, TILES * BLK, LANES)


def from_rows(x):
    return x.reshape(VARS, TILES, BLK, LANES).transpose(2, 0, 1, 3).reshape(BLK, VARS, TILES * LANES)


def field_rows(x):
    return x.reshape(BLK, TILES, LANES).transpose(1, 0, 2).reshape(TILES * BLK, LANES)


def one_hot(count, index):
    places = lax.broadcasted_iota(jnp.int32, (count, index.shape[1]), 0)
    return jnp.where(places == index, 1.0, 0.0).astype(BF16)


def window_of(block, point):
    return ((point >> 6) & 1) * LANES + (point >> 7) * BLK + block


def split(x):
    high = x.astype(BF16)
    return high, (x - high.astype(F32)).astype(BF16)


def interpolate(state_ref, block_ref, point_ref, weight_ref, out_ref, high_ref, low_ref, acc_ref):
    tails = []
    for v in range(VARS):
        turned = state_ref[v].T
        main = jnp.concatenate([turned[:HALF], turned[HALF:]], axis=1)
        high, low = split(main)
        high_ref[v * HALF : (v + 1) * HALF] = high
        low_ref[v * HALF : (v + 1) * HALF] = low
        following = pltpu.roll(turned[:TAIL], LANES - BLK, 1)
        tails.append(jnp.concatenate([turned[HALF : HALF + TAIL], following], axis=1))
    high, low = split(jnp.concatenate(tails, axis=0))
    high_ref[VARS * HALF :] = high
    low_ref[VARS * HALF :] = low
    acc_ref[VARS * SLOTS :] = jnp.zeros((256 - VARS * SLOTS, LANES), F32)
    for first in range(0, SLOTS, GROUP):
        picks, weights = [], []
        for c in range(first, first + GROUP):
            point = point_ref[c : c + 1]
            picks.append(one_hot(256, window_of(block_ref[c : c + 1], point)))
            ahead = lax.broadcasted_iota(jnp.int32, (HALF + TAIL, LANES), 0) - (point & (HALF - 1))
            row = jnp.zeros((HALF + TAIL, LANES), F32)
            for j in range(4):
                row = jnp.where(ahead == j, weight_ref[c, j : j + 1], row)
            weights.append(row)
        pick = jnp.concatenate(picks, axis=1)
        found = jnp.dot(high_ref[...], pick, preferred_element_type=F32)
        found = found + jnp.dot(low_ref[...], pick, preferred_element_type=F32)
        for n, row in enumerate(weights):
            cols = slice(n * LANES, (n + 1) * LANES)
            for v in range(VARS):
                main = found[v * HALF : (v + 1) * HALF, cols] * row[:HALF]
                start = VARS * HALF + v * TAIL
                tail = found[start : start + TAIL, cols] * row[HALF:]
                total = jnp.sum(main, axis=0, keepdims=True) + jnp.sum(tail, axis=0, keepdims=True)
                acc_ref[v * SLOTS + first + n : v * SLOTS + first + n + 1] = total
    out_ref[pl.ds(0, LANES, stride=2), :] = acc_ref[:LANES].T
    out_ref[pl.ds(1, LANES, stride=2), :] = acc_ref[LANES:].T


def product(a, b):
    total = a[:, 0:1] * b[0:1, :]
    for j in range(1, VARS):
        total = total + a[:, j : j + 1] * b[j : j + 1, :]
    return total


def matrices(inv_ref, low_jac_ref, up_jac_ref, order_ref, low_ref, up_ref, mats_ref, square_ref):
    for which, (jac_ref, out_ref) in enumerate(((low_jac_ref, low_ref), (up_jac_ref, up_ref))):
        for i in range(VARS):
            row = inv_ref[i]
            total = row[:, 0:1] * jac_ref[0]
            for j in range(1, VARS):
                total = total + row[:, j : j + 1] * jac_ref[j]
            out_ref[i] = total
        for k in range(BLK):
            for i in range(VARS):
                square_ref[which * BLK + k, i : i + 1, :] = out_ref[i, pl.ds(order_ref[0, k], 1), :]
    low = [square_ref[k] for k in range(BLK)]
    up = [square_ref[BLK + k] for k in range(BLK)]
    downs = [low[0]]
    for k in range(1, BLK):
        downs.append(product(low[k], downs[-1]))
    ups = [up[0]]
    for k in range(1, BLK):
        ups.append(product(ups[-1], up[k]))
    mixed = [downs[0]] + [product(ups[k - 1], downs[k]) for k in range(1, BLK)]
    mats_ref[...] = jnp.zeros_like(mats_ref)
    for m, mat in enumerate([downs[-1], ups[-1]] + mixed):
        mats_ref[0:VARS, m * VARS : (m + 1) * VARS] = mat


def first_kernel(
    state_ref, block_ref, point_ref, weight_ref, inv_ref, low_jac_ref, up_jac_ref, order_ref,
    out_ref, low_ref, up_ref, mats_ref, high_s, low_s, acc_s, square_s,
):
    matrices(inv_ref, low_jac_ref, up_jac_ref, order_ref, low_ref, up_ref, mats_ref, square_s)
    interpolate(state_ref, block_ref, point_ref, weight_ref, out_ref, high_s, low_s, acc_s)


def scatter(got_ref, block_ref, point_ref, added_ref, count_ref, high_s, low_s, left_s, right_s, total_s, counting):
    got = jnp.concatenate(
        [got_ref[pl.ds(0, LANES, stride=2), :].T, got_ref[pl.ds(1, LANES, stride=2), :].T[: VARS * SLOTS - LANES]], axis=0
    )
    high = got.astype(BF16).astype(F32)
    high_s[...] = high
    low_s[...] = got - high
    size = VARS * HALF
    for c in range(SLOTS):
        cols = slice(c * LANES, (c + 1) * LANES)
        point = point_ref[c : c + 1]
        right_s[:, cols] = one_hot(256, window_of(block_ref[c : c + 1], point))
        here = lax.broadcasted_iota(jnp.int32, (HALF, LANES), 0) == (point & (HALF - 1))
        for v in range(VARS):
            row = v * SLOTS + c
            left_s[v * HALF : (v + 1) * HALF, cols] = jnp.where(here, high_s[row : row + 1], 0.0).astype(BF16)
            left_s[size + v * HALF : size + (v + 1) * HALF, cols] = jnp.where(here, low_s[row : row + 1], 0.0).astype(BF16)
        if counting:
            left_s[2 * size :, cols] = jnp.where(here, 1.0, 0.0).astype(BF16)
    total_s[...] = lax.dot_general(left_s[...], right_s[...], (((1,), (1,)), ((), ())), preferred_element_type=F32)

    def turned(x):
        return jnp.concatenate([x[:, :LANES], x[:, LANES:]], axis=0).T

    for v in range(VARS):
        first = total_s[v * HALF : (v + 1) * HALF]
        added_ref[v] = turned(first + total_s[size + v * HALF : size + (v + 1) * HALF])
    if counting:
        count_ref[...] = turned(total_s[2 * size :])


def apply_block(mat_ref, b, xs):
    out = []
    for i in range(VARS):
        total = mat_ref[i, b, 0] * xs[0]
        for j in range(1, VARS):
            total = total + mat_ref[i, b, j] * xs[j]
        out.append(total)
    return out


SPAN = 16


def pick(ref, b, first):
    return ref[pl.ds(b + BLK * first, SPAN, stride=BLK), :]


def solve_kernel(counting, rows, *refs):
    (
        got_ref, block_ref, point_ref, state_ref, forcing_ref, visc_ref, diag_ref, lowc_ref, upc_ref,
        inv_ref, low_ref, up_ref, order_ref, extra_ref,
    ) = refs[:14]
    if counting:
        chunk_ref, z_ref, count_ref = refs[14:17]
        scratch = refs[17:]
    else:
        chunk_ref, z_ref = refs[14:16]
        count_ref = extra_ref
        scratch = refs[16:]
    resid_s, high_s, low_s, left_s, right_s, total_s = scratch
    scatter(got_ref, block_ref, point_ref, resid_s, count_ref, high_s, low_s, left_s, right_s, total_s, counting)
    lane = lax.broadcasted_iota(jnp.int32, (LANES, LANES), 1)
    row = lax.broadcasted_iota(jnp.int32, (LANES, LANES), 0)
    for v in range(VARS):
        x = state_ref[v]
        after = pltpu.roll(x, LANES - 1, 1)
        after = jnp.where(lane == LANES - 1, pltpu.roll(after, LANES - BLK, 0), after)
        after = jnp.where((lane == LANES - 1) & (row >= LANES - BLK), 0.0, after)
        before = pltpu.roll(x, 1, 1)
        before = jnp.where(lane == 0, pltpu.roll(before, BLK, 0), before)
        before = jnp.where((lane == 0) & (row < BLK), 0.0, before)
        flux = visc_ref[...] * (after - 2.0 * x + before)
        resid_s[v] = forcing_ref[v] + flux + (resid_s[v] - count_ref[...] * x)
    if counting:
        for s in range(TILES):
            chunk_ref[s * rows + 16 : s * rows + 24] = extra_ref[...]
    for first in range(0, TILES, SPAN):

        def put(r, value):
            chunk_ref[pl.ds(first * rows + r, SPAN, stride=rows), :] = value

        z, stars, factors = None, [], []
        for k in range(BLK):
            b = order_ref[0, k]
            scale = pick(diag_ref, b, first)
            solved = apply_block(inv_ref, b, [pick(resid_s.at[j], b, first) for j in range(VARS)])
            factor = scale * pick(lowc_ref, b, first)
            if k == 0:
                z = [scale * x for x in solved]
            else:
                moved = apply_block(low_ref, b, z)
                z = [factor * m + scale * x for m, x in zip(moved, solved)]
            for i in range(VARS):
                z_ref[k, i, first : first + SPAN] = z[i]
            factors.append(factor)
        for i in range(VARS):
            put(i, z[i])
        y = z
        for k in reversed(range(BLK - 1)):
            b = order_ref[0, k]
            moved = apply_block(up_ref, b, y)
            factor = pick(upc_ref, b, first)
            y = [z_ref[k, i, first : first + SPAN] + factor * moved[i] for i in range(VARS)]
        for i in range(VARS):
            put(8 + i, y[i])
        if counting:
            down, up = factors[0], pick(upc_ref, order_ref[0, 0], first)
            places = (14, 15, 22, 23)
            put(places[0], down)
            for k in range(1, BLK):
                down = down * factors[k]
                put(places[k], down * up)
                up = up * pick(upc_ref, order_ref[0, k], first)
            put(6, down)
            put(7, up)
        else:
            for r in (6, 7, 14, 15):
                put(r, jnp.zeros((SPAN, LANES), F32))


def chain_kernel(rows, in_ref, coef_ref, out_ref, mid_s):
    def column(tile, m, j):
        at = m * VARS + j
        return jnp.broadcast_to(tile[:, at : at + 1], (8, LANES))

    def spread(x):
        return [jnp.broadcast_to(x[j : j + 1], (8, LANES)) for j in range(VARS)]

    def apply(tile, m, parts):
        terms = [column(tile, m, j) * parts[j] for j in range(VARS)]
        return ((terms[0] + terms[1]) + (terms[2] + terms[3])) + (terms[4] + terms[5])

    count = TILES
    down = jnp.zeros((8, LANES), F32)
    for s in range(count):
        out_ref[16 * s : 16 * s + 8] = down
        tile = coef_ref[24 * s + 16 : 24 * s + 24]
        parts = spread(down)
        mid = in_ref[rows * s + 8 : rows * s + 16]
        for k, place in enumerate((14, 15, 22, 23)):
            mid = mid + coef_ref[24 * s + place : 24 * s + place + 1] * apply(tile, 2 + k, parts)
        mid_s[s] = mid
        down = coef_ref[24 * s + 6 : 24 * s + 7] * apply(tile, 0, parts) + in_ref[rows * s : rows * s + 8]
    up = jnp.zeros((8, LANES), F32)
    for s in reversed(range(count)):
        out_ref[16 * s + 8 : 16 * s + 16] = up
        tile = coef_ref[24 * s + 16 : 24 * s + 24]
        up = coef_ref[24 * s + 7 : 24 * s + 8] * apply(tile, 1, spread(up)) + mid_s[s]


def finish(back_ref, z_ref, state_ref, diag_ref, lowc_ref, upc_ref, low_ref, up_ref, order_ref, new_ref, corr_ref, star_s):
    for first in range(0, TILES, SPAN):
        enter = [back_ref[pl.ds(first * 16 + i, SPAN, stride=16), :] for i in range(VARS)]
        for k in range(BLK):
            b = order_ref[0, k]
            factor = pick(diag_ref, b, first) * pick(lowc_ref, b, first)
            enter = [factor * m for m in apply_block(low_ref, b, enter)]
            for i in range(VARS):
                star_s[k, i, first : first + SPAN] = enter[i] + z_ref[k, i, first : first + SPAN]
        corr = [back_ref[pl.ds(first * 16 + 8 + i, SPAN, stride=16), :] for i in range(VARS)]
        for k in reversed(range(BLK)):
            b = order_ref[0, k]
            factor = pick(upc_ref, b, first)
            moved = apply_block(up_ref, b, corr)
            corr = [star_s[k, i, first : first + SPAN] + factor * moved[i] for i in range(VARS)]
            for i in range(VARS):
                rows = pl.ds(b + BLK * first, SPAN, stride=BLK)
                if corr_ref is not None:
                    corr_ref[i, rows, :] = corr[i]
                new_ref[i, rows, :] = state_ref[i, rows, :] + corr[i]


def middle_kernel(
    back_ref, z_ref, state_ref, diag_ref, lowc_ref, upc_ref, low_ref, up_ref, order_ref,
    block_ref, point_ref, weight_ref, new_ref, out_ref, star_s, high_s, low_s, acc_s,
):
    finish(back_ref, z_ref, state_ref, diag_ref, lowc_ref, upc_ref, low_ref, up_ref, order_ref, new_ref, None, star_s)
    interpolate(new_ref, block_ref, point_ref, weight_ref, out_ref, high_s, low_s, acc_s)


def shape(*dims):
    return jax.ShapeDtypeStruct(dims, F32)


def per_device(
    state, forcing, viscosity, inverses, lower_jac, upper_jac, diag_scale, lower_coupling, upper_coupling,
    donor_block, donor_point, donor_weight, fringe_block, fringe_point, block_order,
):
    big = (VARS, TILES * BLK, LANES)
    state, forcing = to_rows(state[0]), to_rows(forcing[0])
    visc, diag, lowc, upc = (field_rows(x[0]) for x in (viscosity, diag_scale, lower_coupling, upper_coupling))
    inv, low_jac, up_jac = (x[0].transpose(1, 0, 2) for x in (inverses, lower_jac, upper_jac))
    src_block, src_point, dst_block, dst_point = (x[0].T for x in (donor_block, donor_point, fringe_block, fringe_point))
    weight = donor_weight[0].transpose(1, 2, 0)
    sent = VARS * (HALF + TAIL)
    gather_scratch = [pltpu.VMEM((sent, 256), BF16), pltpu.VMEM((sent, 256), BF16), pltpu.VMEM((256, LANES), F32)]

    interp, low, up, mats = pl.pallas_call(
        first_kernel,
        out_shape=[shape(256, LANES), shape(VARS, BLK, VARS), shape(VARS, BLK, VARS), shape(8, LANES)],
        in_specs=[VMEM] * 7 + [SMEM],
        out_specs=[VMEM] * 4,
        scratch_shapes=gather_scratch + [pltpu.VMEM((2 * BLK, VARS, VARS), F32)],
        compiler_params=PARAMS,
        name="first",
    )(state, src_block, src_point, weight, inv, low_jac, up_jac, block_order)

    def exchange(x, axes, count):
        parts = x.reshape(count, -1, LANES)
        return lax.all_to_all(parts, axes, split_axis=0, concat_axis=0, tiled=True).reshape(x.shape)

    def solve(counting, got, state, extra):
        rows = 24 if counting else 16
        left = (2 * VARS + counting) * HALF
        outs = [shape(TILES * rows, LANES), shape(BLK, VARS, TILES, LANES)] + [shape(LANES, LANES)] * counting
        return pl.pallas_call(
            lambda *refs: solve_kernel(counting, rows, *refs),
            out_shape=outs,
            in_specs=[VMEM] * 9 + [SMEM] * 4 + [VMEM],
            out_specs=[VMEM] * len(outs),
            scratch_shapes=[
                pltpu.VMEM(big, F32),
                pltpu.VMEM((VARS * SLOTS, LANES), F32),
                pltpu.VMEM((VARS * SLOTS, LANES), F32),
                pltpu.VMEM((left, SLOTS * LANES), BF16),
                pltpu.VMEM((256, SLOTS * LANES), BF16),
                pltpu.VMEM((left, 256), F32),
            ],
            compiler_params=PARAMS,
            name="solve",
        )(got, dst_block, dst_point, state, forcing, visc, diag, lowc, upc, inv, low, up, block_order, extra)

    def chain(values, coefs):
        return pl.pallas_call(
            lambda *refs: chain_kernel(values.shape[0] // TILES, *refs),
            out_shape=shape(TILES * 16, LANES),
            in_specs=[VMEM] * 2,
            out_specs=VMEM,
            scratch_shapes=[pltpu.VMEM((TILES, 8, LANES), F32)],
            compiler_params=PARAMS,
            name="chain",
        )(values, coefs)

    got = exchange(interp, ("sweep", "grp"), 128)
    chunk, z, count = solve(True, got, state, mats)
    coefs = exchange(chunk, "sweep", TILES)
    back = exchange(chain(coefs, coefs), "sweep", TILES)
    star_scratch = pltpu.VMEM((BLK, VARS, TILES, LANES), F32)
    state, interp = pl.pallas_call(
        middle_kernel,
        out_shape=[shape(*big), shape(256, LANES)],
        in_specs=[VMEM] * 6 + [SMEM] * 3 + [VMEM] * 3,
        out_specs=[VMEM] * 2,
        scratch_shapes=[star_scratch] + gather_scratch,
        compiler_params=PARAMS,
        name="middle",
    )(back, z, state, diag, lowc, upc, low, up, block_order, src_block, src_point, weight)
    got = exchange(interp, ("sweep", "grp"), 128)
    chunk, z = solve(False, got, state, count)
    back = exchange(chain(exchange(chunk, "sweep", TILES), coefs), "sweep", TILES)
    state, correction = pl.pallas_call(
        finish,
        out_shape=[shape(*big), shape(*big)],
        in_specs=[VMEM] * 6 + [SMEM] * 3,
        out_specs=[VMEM] * 2,
        scratch_shapes=[star_scratch],
        compiler_params=PARAMS,
        name="finish",
    )(back, z, state, diag, lowc, upc, low, up, block_order)
    return from_rows(state)[None], from_rows(correction)[None]


def solution(mesh):
    blocks = P("grp", "sweep", None, None)
    field = P("grp", "sweep", None)
    table = P(("sweep", "grp"), None, None)
    return jax.shard_map(
        per_device,
        mesh=mesh,
        in_specs=(
            blocks, blocks, field, blocks, blocks, blocks, field, field, field,
            table, table, P(("sweep", "grp"), None, None, None), table, table, P("grp", "sweep"),
        ),
        out_specs=(blocks, blocks),
        check_vma=False,
    )
```

time: 1590 us -> 119 us (0.07)
  the two profiles are of different devices: /device:TPU:7 before, /device:TPU:1 now
where the time goes in v1:
time: 119 us; the launch traced here: 118 us
  blocking collectives  86.6 us (73%)
  Pallas kernels  24.4 us (21%)
  local copies, waits for them, and re-layouts  6.1 us (5%)
    all_to_all x6, blocking collectives, exchange(): lax.all_to_all(parts, axes, split_axis=0, concat_axis=0, tiled=True)  86.6 us
    pallas_call x2, Pallas kernels, solve(): pl.pallas_call(lambda *refs: solve_kernel(counting, rows, *refs), out_sha...  10.7 us
    unnamed x34, local copies, waits for them, and re-layouts  6.1 us
    pallas_call x2, Pallas kernels, chain(): pl.pallas_call(lambda *refs: chain_kernel(values.shape[0] // TILES, *refs...  4.07 us
    pallas_call x1, Pallas kernels, per_device(): pl.pallas_call(middle_kernel, out_shape=[shape(*big), shape(256, LANES)],...  4.01 us
    pallas_call x1, Pallas kernels, per_device(): pl.pallas_call(first_kernel, out_shape=[shape(256, LANES), shape(VARS, BL...  3.14 us
    pallas_call x1, Pallas kernels, per_device(): pl.pallas_call(finish, out_shape=[shape(*big), shape(*big)], in_specs=[VM...  2.45 us

profile of v1, /device:TPU:1, one launch (start us, length us, event | category | flops | bytes accessed | tf_op | source)
XLA Modules:
  0.0 117.9 jit_solution(7278008020721828812)
XLA Ops:
  0.6 0.0 copy-start.8
  0.6 0.0 copy-start.14
  0.7 0.7 copy-done.8
  1.3 0.0 copy-done.14
  1.3 1.0 copy-done
  2.3 0.8 copy-done.5
  3.2 0.7 copy-done.11
  3.9 0.7 copy-done.13
  4.6 0.7 copy-done.15
  5.3 0.7 copy-done.16
  6.0 3.1 %first.1 = (f32[256,128]{1,0:T(8,128)S(1)}, f32[6,4,6]{2,1,0:T(4,128)S(1)}, f32[6,4,6]{2,1,0:T(4,128)S(1)}, f32[8,128]{1,0:T(8,128)S(1)}) custom-call(f32[6,128,128]{2,1,0:T(8,128)S(1)} %bitcast.79, s32[32,128]{1,0:T(8,128)S(1)} %bitcast.118, s32[32,128]{1,0:T(8,128)S(1)} %bitcast.120, f32[32,4,128]{2,1,0:T(4,128)S(1)} %bitcast.104, ...), custom_call_target="tpu_custom_call" | custom-call | tf_op jit(solution)/shard_map/first/pallas_call | solution.py:326
  9.2 0.0 copy-start.2
  9.2 0.0 copy-start.3
  9.2 0.0 copy-start.4
  9.2 0.0 copy-start.7
  9.2 21.6 %all_to_all.30 = f32[128,2,128]{2,1,0:T(2,128)S(1)} all-to-all(f32[128,2,128]{2,1,0:T(2,128)S(1)} %bitcast.109), channel_id=1, replica_groups=mesh['sweep'=32,'grp'=4] {'sweep','grp'}, dimensions={0} | all-to-all | bytes 262144 | tf_op jit(solution)/shard_map/all_to_all | solution.py:338
  30.8 0.0 copy-done.1
  30.8 0.7 copy-done.9
  31.5 5.4 %solve.2 = (f32[768,128]{1,0:T(8,128)S(1)}, f32[4,6,32,128]{3,2,1,0:T(8,128)S(1)}, f32[128,128]{1,0:T(8,128)S(1)}) custom-call(f32[256,128]{1,0:T(8,128)S(1)} %bitcast.101, s32[32,128]{1,0:T(8,128)S(1)} %bitcast.114, s32[32,128]{1,0:T(8,128)S(1)} %bitcast.116, f32[6,128,128]{2,1,0:T(8,128)S(1)} %bitcast.80, f32[6,128,128]{2,1,0:T(8,128)S(1)} %bitcast.82, ...), custom_call_target="tpu_custom_call" | custom-call | tf_op jit(solution)/shard_map/solve/pallas_call | solution.py:344
  36.9 13.6 %all_to_all.31 = f32[32,24,128]{2,1,0:T(8,128)S(1)} all-to-all(f32[32,24,128]{2,1,0:T(8,128)S(1)} %bitcast.103), channel_id=1, replica_groups=mesh['sweep'=32,'grp'=4] {'sweep'}, dimensions={0} | all-to-all | bytes 786432 | tf_op jit(solution)/shard_map/all_to_all | solution.py:338
  50.5 2.0 %chain.2 = f32[512,128]{1,0:T(8,128)S(1)} custom-call(f32[768,128]{1,0:T(8,128)S(1)} %bitcast.76, f32[768,128]{1,0:T(8,128)S(1)} %bitcast.77), custom_call_target="tpu_custom_call" | custom-call | tf_op jit(solution)/shard_map/chain/pallas_call | solution.py:362
  52.5 0.0 copy-start.6
  52.6 0.0 copy-start.12
  52.6 12.6 %all_to_all.32 = f32[32,16,128]{2,1,0:T(8,128)S(1)} all-to-all(f32[32,16,128]{2,1,0:T(8,128)S(1)} %bitcast.100), channel_id=1, replica_groups=mesh['sweep'=32,'grp'=4] {'sweep'}, dimensions={0} | all-to-all | bytes 524288 | tf_op jit(solution)/shard_map/all_to_all | solution.py:338
  65.2 0.0 copy-done.12
  65.2 4.0 %middle.1 = (f32[6,128,128]{2,1,0:T(8,128)S(1)}, f32[256,128]{1,0:T(8,128)S(1)}) custom-call(f32[512,128]{1,0:T(8,128)S(1)} %bitcast.96, f32[4,6,32,128]{3,2,1,0:T(8,128)S(1)} %get-tuple-element.20.z_ref, f32[6,128,128]{2,1,0:T(8,128)S(1)} %bitcast.81, f32[128,128]{1,0:T(8,128)S(1)} %bitcast.85, f32[128,128]{1,0:T(8,128)S(1)} %bitcast.89, ...), custom_call_target="tpu_custom_call" | custom-call | tf_op jit(solution)/shard_map/middle/pallas_call | solution.py:377
  69.2 14.1 %all_to_all.33 = f32[128,2,128]{2,1,0:T(2,128)S(1)} all-to-all(f32[128,2,128]{2,1,0:T(2,128)S(1)} %bitcast.110), channel_id=1, replica_groups=mesh['sweep'=32,'grp'=4] {'sweep','grp'}, dimensions={0} | all-to-all | bytes 262144 | tf_op jit(solution)/shard_map/all_to_all | solution.py:338
  83.3 5.3 %solve.3 = (f32[512,128]{1,0:T(8,128)S(1)}, f32[4,6,32,128]{3,2,1,0:T(8,128)S(1)}) custom-call(f32[256,128]{1,0:T(8,128)S(1)} %bitcast.102, s32[32,128]{1,0:T(8,128)S(1)} %bitcast.115, s32[32,128]{1,0:T(8,128)S(1)} %bitcast.117, f32[6,128,128]{2,1,0:T(8,128)S(1)} %get-tuple-element.22.refs_3_.state_ref, f32[6,128,128]{2,1,0:T(8,128)S(1)} %bitcast.83, ...), custom_call_target="tpu_custom_call" | custom-call | tf_op jit(solution)/shard_map/solve/pallas_call | solution.py:344
  88.6 12.3 %all_to_all.34 = f32[32,16,128]{2,1,0:T(8,128)S(1)} all-to-all(f32[32,16,128]{2,1,0:T(8,128)S(1)} %bitcast.108), channel_id=1, replica_groups=mesh['sweep'=32,'grp'=4] {'sweep'}, dimensions={0} | all-to-all | bytes 524288 | tf_op jit(solution)/shard_map/all_to_all | solution.py:338
  100.9 2.0 %chain.3 = f32[512,128]{1,0:T(8,128)S(1)} custom-call(f32[512,128]{1,0:T(8,128)S(1)} %bitcast.97, f32[768,128]{1,0:T(8,128)S(1)} %bitcast.78), custom_call_target="tpu_custom_call" | custom-call | tf_op jit(solution)/shard_map/chain/pallas_call | solution.py:362
  103.0 12.5 %all_to_all.35 = f32[32,16,128]{2,1,0:T(8,128)S(1)} all-to-all(f32[32,16,128]{2,1,0:T(8,128)S(1)} %bitcast.98), channel_id=1, replica_groups=mesh['sweep'=32,'grp'=4] {'sweep'}, dimensions={0} | all-to-all | bytes 524288 | tf_op jit(solution)/shard_map/all_to_all | solution.py:338
  115.4 2.5 %finish.1 = (f32[6,128,128]{2,1,0:T(8,128)}, f32[6,128,128]{2,1,0:T(8,128)}) custom-call(f32[512,128]{1,0:T(8,128)S(1)} %bitcast.99, f32[4,6,32,128]{3,2,1,0:T(8,128)S(1)} %get-tuple-element.25.z_ref, f32[6,128,128]{2,1,0:T(8,128)S(1)} %get-tuple-element.22.refs_3_.state_ref, f32[128,128]{1,0:T(8,128)S(1)} %bitcast.87, f32[128,128]{1,0:T(8,128)S(1)} %bitcast.91, ...), custom_call_target="tpu_custom_call" | custom-call | tf_op jit(solution)/shard_map/finish/pallas_call | solution.py:389
  (15 shorter events, 0.0 us)
Async XLA Ops:
  0.6 0.7 copy-start.8
  0.6 0.7 copy-start.14
  1.3 1.0 copy-start
  2.3 0.8 copy-start.5
  3.2 0.7 copy-start.11
  3.9 0.7 copy-start.13
  4.6 0.7 copy-start.15
  5.3 0.7 copy-start.16
  6.0 24.8 %copy-start.1 = (f32[1,4,6,4096]{3,1,2,0:T(4,128)S(1)}, f32[1,4,6,4096]{3,1,2,0:T(4,128)}, u32[]{:S(2)}) copy-start(f32[1,4,6,4096]{3,1,2,0:T(4,128)} %param.16) | copy-start | bytes 1179652
  6.0 24.8 %copy-start.10 = (s32[1,128,32]{1,2,0:T(8,128)S(1)}, s32[1,128,32]{1,2,0:T(8,128)}, u32[]{:S(2)}) copy-start(s32[1,128,32]{1,2,0:T(8,128)} %param.28) | copy-start | bytes 49156
  9.2 21.6 %copy-start.2 = (f32[1,4,4096]{2,1,0:T(4,128)S(1)}, f32[1,4,4096]{2,1,0:T(4,128)}, u32[]{:S(2)}) copy-start(f32[1,4,4096]{2,1,0:T(4,128)} %param.21) | copy-start | bytes 196612
  9.2 21.6 %copy-start.3 = (f32[1,4,4096]{2,1,0:T(4,128)S(1)}, f32[1,4,4096]{2,1,0:T(4,128)}, u32[]{:S(2)}) copy-start(f32[1,4,4096]{2,1,0:T(4,128)} %param.22) | copy-start | bytes 196612
  9.2 21.6 %copy-start.4 = (f32[1,4,4096]{2,1,0:T(4,128)S(1)}, f32[1,4,4096]{2,1,0:T(4,128)}, u32[]{:S(2)}) copy-start(f32[1,4,4096]{2,1,0:T(4,128)} %param.23) | copy-start | bytes 196612
  9.2 21.6 %copy-start.7 = (f32[1,4,4096]{2,1,0:T(4,128)S(1)}, f32[1,4,4096]{2,1,0:T(4,128)}, u32[]{:S(2)}) copy-start(f32[1,4,4096]{2,1,0:T(4,128)} %param.17) | copy-start | bytes 196612
  30.8 0.7 copy-start.9
  52.5 12.6 %copy-start.6 = (f32[1,128,32,4]{1,3,2,0:T(4,128)S(1)}, f32[1,128,32,4]{1,3,2,0:T(4,128)}, u32[]{:S(2)}) copy-start(f32[1,128,32,4]{1,3,2,0:T(4,128)} %param.26) | copy-start | bytes 196612
  52.6 12.6 %copy-start.12 = (s32[1,128,32]{1,2,0:T(8,128)S(1)}, s32[1,128,32]{1,2,0:T(8,128)}, u32[]{:S(2)}) copy-start(s32[1,128,32]{1,2,0:T(8,128)} %param.24) | copy-start | bytes 49156

commit v2 on v1

v2 whole, which is shorter than its diff:
```python
import jax
import jax.numpy as jnp
from jax import lax
from jax.experimental import pallas as pl
from jax.experimental.pallas import tpu as pltpu
from jax.sharding import PartitionSpec as P

F32 = jnp.float32
BF16 = jnp.bfloat16
VARS = 6
BLK = 4
TILES = 32
SLOTS = 32
LANES = 128
ROWS = TILES * BLK
HALF = 64
TAIL = 8
GROUP = 4
BATCH = 8
SPAN = 16
SQUARE = VARS * VARS
INV, LOW, UP = 0, 1, 2
DIAG, DOWN, RISE = 0, 1, 2
FULL = 20
BARE = 12
VMEM = pl.BlockSpec(memory_space=pltpu.VMEM)
PARAMS = pltpu.CompilerParams(vmem_limit_bytes=24 * 1024 * 1024)
BESIDE = pl.CostEstimate(flops=20_000_000_000, bytes_accessed=4_000_000, transcendentals=0)


def to_rows(x):
    return x.reshape(BLK, VARS, TILES, LANES).transpose(1, 2, 0, 3).reshape(VARS, ROWS, LANES)


def from_rows(x):
    return x.reshape(VARS, TILES, BLK, LANES).transpose(2, 0, 1, 3).reshape(BLK, VARS, TILES * LANES)


def field_rows(x):
    return x.reshape(BLK, TILES, LANES).transpose(1, 0, 2).reshape(ROWS, LANES)


def one_hot(count, index):
    places = lax.broadcasted_iota(jnp.int32, (count, index.shape[1]), 0)
    return jnp.where(places == index, 1.0, 0.0).astype(BF16)


def window_of(block, point):
    return ((point >> 6) & 1) * LANES + (point >> 7) * BLK + block


def split(x):
    high = x.astype(BF16)
    return high, (x - high.astype(F32)).astype(BF16)


def order_of(order_ref):
    order = order_ref[...]
    return [order[0, k] for k in range(BLK)]


def windows(state_ref, high_ref, low_ref):
    tails = []
    for v in range(VARS):
        turned = state_ref[v].T
        high, low = split(jnp.concatenate([turned[:HALF], turned[HALF:]], axis=1))
        high_ref[v * HALF : (v + 1) * HALF] = high
        low_ref[v * HALF : (v + 1) * HALF] = low
        following = pltpu.roll(turned[:TAIL], LANES - BLK, 1)
        tails.append(jnp.concatenate([turned[HALF : HALF + TAIL], following], axis=1))
    high, low = split(jnp.concatenate(tails, axis=0))
    high_ref[VARS * HALF :] = high
    low_ref[VARS * HALF :] = low


def stencil_of(point, weight_ref, c):
    ahead = lax.broadcasted_iota(jnp.int32, (HALF + TAIL, LANES), 0) - (point & (HALF - 1))
    row = jnp.zeros((HALF + TAIL, LANES), F32)
    for j in range(4):
        row = jnp.where(ahead == j, weight_ref[c, j : j + 1], row)
    return row


def gather(block_ref, point_ref, weight_ref, out_ref, high_ref, low_ref, acc_ref):
    acc_ref[VARS * SLOTS :] = jnp.zeros((256 - VARS * SLOTS, LANES), F32)
    for first in range(0, SLOTS, GROUP):
        picks = []
        for c in range(first, first + GROUP):
            picks.append(one_hot(256, window_of(block_ref[c : c + 1], point_ref[c : c + 1])))
        pick = jnp.concatenate(picks, axis=1)
        found = jnp.dot(high_ref[...], pick, preferred_element_type=F32)
        found = found + jnp.dot(low_ref[...], pick, preferred_element_type=F32)
        for n in range(GROUP):
            cols = slice(n * LANES, (n + 1) * LANES)
            row = stencil_of(point_ref[first + n : first + n + 1], weight_ref, first + n)
            for v in range(VARS):
                main = found[v * HALF : (v + 1) * HALF, cols] * row[:HALF]
                start = VARS * HALF + v * TAIL
                tail = found[start : start + TAIL, cols] * row[HALF:]
                total = jnp.sum(main, axis=0, keepdims=True) + jnp.sum(tail, axis=0, keepdims=True)
                acc_ref[v * SLOTS + first + n : v * SLOTS + first + n + 1] = total
    out_ref[pl.ds(0, LANES, stride=2), :] = acc_ref[:LANES].T
    out_ref[pl.ds(1, LANES, stride=2), :] = acc_ref[LANES:].T


def fetch(pairs, sems):
    copies = [pltpu.make_async_copy(src, dst, sems.at[n]) for n, (src, dst) in enumerate(pairs)]
    for copy in copies:
        copy.start()
    return copies


def first_kernel(
    block_hbm, point_hbm, state_hbm, weight_hbm, out_ref, state_ref, block_s, point_s, weight_s, high_s, low_s, acc_s, sems
):
    pairs = ((block_hbm, block_s), (point_hbm, point_s), (state_hbm, state_ref), (weight_hbm, weight_s))
    for copy in fetch(pairs, sems):
        copy.wait()
    windows(state_ref, high_s, low_s)
    gather(block_s, point_s, weight_s, out_ref, high_s, low_s, acc_s)


def product(a, b):
    total = a[:, 0:1] * b[0:1, :]
    for j in range(1, VARS):
        total = total + a[:, j : j + 1] * b[j : j + 1, :]
    return total


def matrices(inv_ref, low_jac_ref, up_jac_ref, order, wide_ref, maps_ref, native_s, square_s, spread_s, mats_s):
    for i in range(VARS):
        row = inv_ref[i]
        native_s[INV, i] = row
        for which, jac_ref in ((LOW, low_jac_ref), (UP, up_jac_ref)):
            total = row[:, 0:1] * jac_ref[0]
            for j in range(1, VARS):
                total = total + row[:, j : j + 1] * jac_ref[j]
            native_s[which, i] = total
    for which in (INV, LOW, UP):
        for i in range(VARS):
            row = native_s[which, i]
            for j in range(VARS):
                at = ((which * VARS + i) * VARS + j) * BLK
                spread_s[at : at + BLK] = jnp.broadcast_to(row[:, j : j + 1], (BLK, LANES))
    for k in range(BLK):
        wide_ref[k] = spread_s[pl.ds(order[k], 3 * SQUARE, stride=BLK), :]
        for which in (LOW, UP):
            for i in range(VARS):
                square_s[which * BLK + k, i : i + 1, :] = native_s[which, i, pl.ds(order[k], 1), :]
    low = [square_s[LOW * BLK + k] for k in range(BLK)]
    up = [square_s[UP * BLK + k] for k in range(BLK)]
    downs, ups = [low[0]], [up[0]]
    for k in range(1, BLK):
        downs.append(product(low[k], downs[-1]))
        ups.append(product(ups[-1], up[k]))
    mixed = [downs[0]] + [product(ups[k - 1], downs[k]) for k in range(1, BLK)]
    mats_s[...] = jnp.zeros_like(mats_s)
    for m, mat in enumerate([downs[-1], ups[-1]] + mixed):
        mats_s[0:VARS, m * VARS : (m + 1) * VARS] = mat
    mats = mats_s[...]
    for half in range(2):
        line = mats[3 * half : 3 * half + 1]
        for n in (1, 2):
            line = line + pltpu.roll(mats[3 * half + n : 3 * half + n + 1], n * SQUARE, 1)
        maps_ref[6 + half] = jnp.broadcast_to(line, (TILES, LANES))


def residual(state_ref, forcing_ref, visc_ref, count_ref, out_ref):
    count = count_ref[...]
    lane = lax.broadcasted_iota(jnp.int32, (ROWS, LANES), 1)
    row = lax.broadcasted_iota(jnp.int32, (ROWS, LANES), 0)
    for v in range(VARS):
        x = state_ref[v]
        after = pltpu.roll(x, LANES - 1, 1)
        after = jnp.where(lane == LANES - 1, pltpu.roll(after, ROWS - BLK, 0), after)
        after = jnp.where((lane == LANES - 1) & (row >= ROWS - BLK), 0.0, after)
        before = pltpu.roll(x, 1, 1)
        before = jnp.where(lane == 0, pltpu.roll(before, BLK, 0), before)
        before = jnp.where((lane == 0) & (row < BLK), 0.0, before)
        out_ref[v] = forcing_ref[v] + visc_ref[...] * (after - 2.0 * x + before) + (out_ref[v] - count * x)


def turned(x):
    return jnp.concatenate([x[:, :LANES], x[:, LANES:]], axis=0).T


def contract(left, right):
    return lax.dot_general(left, right, (((1,), (1,)), ((), ())), preferred_element_type=F32)


def base_kernel(
    block_hbm, point_hbm, diag_hbm, lowc_hbm, upc_hbm, inv_hbm, low_jac_hbm, up_jac_hbm, order_hbm,
    place_ref, count_ref, wide_ref, factor_ref, maps_ref, point_ref, order_ref,
    block_ref, diag_ref, lowc_ref, upc_ref, inv_ref, low_jac_ref, up_jac_ref,
    left_s, native_s, square_s, spread_s, mats_s, sems,
):
    pairs = (
        (block_hbm, block_ref), (point_hbm, point_ref), (order_hbm, order_ref), (inv_hbm, inv_ref),
        (low_jac_hbm, low_jac_ref), (up_jac_hbm, up_jac_ref), (diag_hbm, diag_ref), (lowc_hbm, lowc_ref),
        (upc_hbm, upc_ref),
    )
    for copy in fetch(pairs, sems):
        copy.wait()
    order = order_of(order_ref)
    for c in range(SLOTS):
        cols = slice(c * LANES, (c + 1) * LANES)
        point = point_ref[c : c + 1]
        place_ref[:, cols] = one_hot(256, window_of(block_ref[c : c + 1], point))
        left_s[:, cols] = one_hot(HALF, point & (HALF - 1))
    matrices(inv_ref, low_jac_ref, up_jac_ref, order, wide_ref, maps_ref, native_s, square_s, spread_s, mats_s)
    down = up = None
    for k in range(BLK):
        rows = pl.ds(order[k], TILES, stride=BLK)
        scale = diag_ref[rows, :]
        fall, rise = scale * lowc_ref[rows, :], upc_ref[rows, :]
        factor_ref[DIAG * BLK + k] = scale
        factor_ref[DOWN * BLK + k] = fall
        factor_ref[RISE * BLK + k] = rise
        down = fall if k == 0 else down * fall
        maps_ref[2 + k] = down if k == 0 else down * up
        up = rise if k == 0 else up * rise
    maps_ref[0] = down
    maps_ref[1] = up
    count_ref[...] = turned(contract(left_s[...], place_ref[...]))


def scatter(got_ref, point_ref, place_ref, out_ref, high_s, low_s, total_s):
    high_s[:LANES] = got_ref[pl.ds(0, LANES, stride=2), :].T
    high_s[LANES:] = got_ref[pl.ds(1, LANES, stride=2), :].T[: VARS * SLOTS - LANES]
    got = high_s[...]
    high = got.astype(BF16).astype(F32)
    high_s[...] = high
    low_s[...] = got - high
    for first in range(0, SLOTS, BATCH):
        parts = []
        for c in range(first, first + BATCH):
            here = lax.broadcasted_iota(jnp.int32, (HALF, LANES), 0) == (point_ref[c : c + 1] & (HALF - 1))
            pieces = []
            for ref in (high_s, low_s):
                for v in range(VARS):
                    pieces.append(jnp.where(here, ref[v * SLOTS + c : v * SLOTS + c + 1], 0.0).astype(BF16))
            parts.append(jnp.concatenate(pieces, axis=0))
        left = jnp.concatenate(parts, axis=1)
        total = contract(left, place_ref[:, first * LANES : (first + BATCH) * LANES])
        if first == 0:
            total_s[...] = total
        else:
            total_s[...] += total
    size = VARS * HALF
    for v in range(VARS):
        added = total_s[v * HALF : (v + 1) * HALF] + total_s[size + v * HALF : size + (v + 1) * HALF]
        out_ref[v] = turned(added)


def apply_block(wide_ref, k, which, xs):
    out = []
    for i in range(VARS):
        at = which * SQUARE + i * VARS
        total = wide_ref[k, at : at + 1] * xs[0]
        for j in range(1, VARS):
            total = total + wide_ref[k, at + j : at + j + 1] * xs[j]
        out.append(total)
    return out


def factor_at(factor_ref, which, k, first):
    return factor_ref[which * BLK + k, first : first + SPAN]


def solve_kernel(full, *refs):
    rows = FULL if full else BARE
    got_ref, point_ref, place_ref, wide_ref, factor_ref, order_ref, count_ref, state_ref, visc_hbm, forcing_hbm = refs[:10]
    refs = refs[10:]
    if full:
        maps_ref, refs = refs[0], refs[1:]
    chunk_ref, z_ref, resid_s, high_s, low_s, total_s, visc_s, forcing_s, sems = refs
    copies = fetch(((visc_hbm, visc_s), (forcing_hbm, forcing_s)), sems)
    order = order_of(order_ref)
    scatter(got_ref, point_ref, place_ref, resid_s, high_s, low_s, total_s)
    for copy in copies:
        copy.wait()
    residual(state_ref, forcing_s, visc_s, count_ref, resid_s)
    if full:
        for r in range(FULL - BARE):
            chunk_ref[pl.ds(BARE + r, TILES, stride=rows), :] = maps_ref[r]
    for first in range(0, TILES, SPAN):

        def put(r, value):
            chunk_ref[pl.ds(first * rows + r, SPAN, stride=rows), :] = value

        z = None
        for k in range(BLK):
            places = pl.ds(order[k] + BLK * first, SPAN, stride=BLK)
            scale = factor_at(factor_ref, DIAG, k, first)
            solved = [scale * x for x in apply_block(wide_ref, k, INV, [resid_s[j, places, :] for j in range(VARS)])]
            if k > 0:
                fall = factor_at(factor_ref, DOWN, k, first)
                solved = [fall * m + x for m, x in zip(apply_block(wide_ref, k, LOW, z), solved)]
            z = solved
            for i in range(VARS):
                z_ref[k, i, first : first + SPAN] = z[i]
        for i in range(VARS):
            put(i, z[i])
        y = z
        for k in reversed(range(BLK - 1)):
            rise = factor_at(factor_ref, RISE, k, first)
            moved = apply_block(wide_ref, k, UP, y)
            y = [z_ref[k, i, first : first + SPAN] + rise * moved[i] for i in range(VARS)]
        for i in range(VARS):
            put(VARS + i, y[i])


def chain_kernel(rows, in_ref, coef_ref, out_ref, value_s, mid_s, mats_s):
    for half in range(2):
        lines = coef_ref[pl.ds(FULL - 2 + half, TILES, stride=FULL), :]
        for n in range(3):
            shifted = pltpu.roll(lines, LANES - n * SQUARE, 1) if n else lines
            mats_s[pl.ds(3 * half + n, TILES, stride=8), :] = shifted
        for i in range(VARS):
            to = value_s if half == 0 else mid_s
            to[pl.ds(i, TILES, stride=8), :] = in_ref[pl.ds(half * VARS + i, TILES, stride=rows), :]

    def apply(mats, m, x):
        terms = []
        for j in range(VARS):
            at = m * VARS + j
            column = jnp.broadcast_to(mats[:, at : at + 1], (VARS, LANES))
            terms.append(column * x[j])
        return ((terms[0] + terms[1]) + (terms[2] + terms[3])) + (terms[4] + terms[5])

    def spread(x):
        return [jnp.broadcast_to(x[j : j + 1], (VARS, LANES)) for j in range(VARS)]

    def coef(s, r):
        return coef_ref[FULL * s + BARE + r : FULL * s + BARE + r + 1]

    down = jnp.zeros((VARS, LANES), F32)
    for s in range(TILES):
        here = slice(8 * s, 8 * s + VARS)
        mats = mats_s[here]
        parts = spread(down)
        mid = mid_s[here]
        for k in range(BLK):
            mid = mid + coef(s, 2 + k) * apply(mats, 2 + k, parts)
        mid_s[here] = mid
        after = coef(s, 0) * apply(mats, 0, parts) + value_s[here]
        value_s[here] = down
        down = after
    up = jnp.zeros((VARS, LANES), F32)
    for s in reversed(range(TILES)):
        here = slice(8 * s, 8 * s + VARS)
        after = coef(s, 1) * apply(mats_s[here], 1, spread(up)) + mid_s[here]
        mid_s[here] = up
        up = after
    for i in range(VARS):
        out_ref[pl.ds(i, TILES, stride=BARE), :] = value_s[pl.ds(i, TILES, stride=8), :]
        out_ref[pl.ds(VARS + i, TILES, stride=BARE), :] = mid_s[pl.ds(i, TILES, stride=8), :]


def finish(back_ref, z_ref, state_ref, wide_ref, factor_ref, order_ref, new_ref, corr_ref, star_s):
    order = order_of(order_ref)
    for first in range(0, TILES, SPAN):
        here = slice(first, first + SPAN)
        enter = [back_ref[pl.ds(first * BARE + i, SPAN, stride=BARE), :] for i in range(VARS)]
        for k in range(BLK):
            fall = factor_at(factor_ref, DOWN, k, first)
            enter = [fall * m for m in apply_block(wide_ref, k, LOW, enter)]
            for i in range(VARS):
                star_s[k, i, here] = enter[i] + z_ref[k, i, here]
        corr = [back_ref[pl.ds(first * BARE + VARS + i, SPAN, stride=BARE), :] for i in range(VARS)]
        for k in reversed(range(BLK)):
            rise = factor_at(factor_ref, RISE, k, first)
            moved = apply_block(wide_ref, k, UP, corr)
            corr = [star_s[k, i, here] + rise * moved[i] for i in range(VARS)]
            places = pl.ds(order[k] + BLK * first, SPAN, stride=BLK)
            for i in range(VARS):
                if corr_ref is not None:
                    corr_ref[i, places, :] = corr[i]
                new_ref[i, places, :] = state_ref[i, places, :] + corr[i]


def middle_kernel(
    back_ref, z_ref, state_ref, wide_ref, factor_ref, order_ref, block_hbm, point_hbm, weight_hbm, new_ref, out_ref,
    star_s, block_s, point_s, weight_s, high_s, low_s, acc_s, sems,
):
    copies = fetch(((block_hbm, block_s), (point_hbm, point_s), (weight_hbm, weight_s)), sems)
    finish(back_ref, z_ref, state_ref, wide_ref, factor_ref, order_ref, new_ref, None, star_s)
    windows(new_ref, high_s, low_s)
    for copy in copies:
        copy.wait()
    gather(block_s, point_s, weight_s, out_ref, high_s, low_s, acc_s)


def shape(*dims, dtype=F32):
    return pltpu.VMEM(dims, dtype)


def call(kernel, name, outs, operands, scratch=(), outside=(), beside=False):
    spaces = [pltpu.HBM if n in outside else pltpu.VMEM for n in range(len(operands))]
    return pl.pallas_call(
        kernel,
        out_shape=outs,
        in_specs=[pl.BlockSpec(memory_space=space) for space in spaces],
        out_specs=[VMEM] * len(outs),
        scratch_shapes=list(scratch),
        compiler_params=PARAMS,
        cost_estimate=BESIDE if beside else None,
        name=name,
    )(*[pltpu.with_memory_space_constraint(x, pltpu.HBM) if n in outside else x for n, x in enumerate(operands)])


def exchange(x, axes, count):
    parts = x.reshape(count, 1, -1)
    return lax.all_to_all(parts, axes, split_axis=0, concat_axis=0, tiled=True).reshape(x.shape)


def per_device(
    state, forcing, viscosity, inverses, lower_jac, upper_jac, diag_scale, lower_coupling, upper_coupling,
    donor_block, donor_point, donor_weight, fringe_block, fringe_point, block_order,
):
    big = (VARS, ROWS, LANES)
    state, forcing = to_rows(state[0]), to_rows(forcing[0])
    visc, diag, lowc, upc = (field_rows(x[0]) for x in (viscosity, diag_scale, lower_coupling, upper_coupling))
    inv, low_jac, up_jac = (x[0].transpose(1, 0, 2) for x in (inverses, lower_jac, upper_jac))
    src_block, src_point, dst_block, dst_point = (x[0].T for x in (donor_block, donor_point, fringe_block, fringe_point))
    weight = donor_weight[0].transpose(1, 2, 0)
    sent = VARS * (HALF + TAIL)
    gather_scratch = [pltpu.VMEM((sent, 256), BF16), pltpu.VMEM((sent, 256), BF16), pltpu.VMEM((256, LANES), F32)]
    star_scratch = [pltpu.VMEM((BLK, VARS, TILES, LANES), F32)]
    chain_scratch = [pltpu.VMEM((TILES * 8, LANES), F32) for _ in range(3)]
    dma = pltpu.SemaphoreType.DMA

    def alike(x):
        return pltpu.VMEM(x.shape, x.dtype)

    source = (src_block, src_point, weight)
    source_scratch = [alike(x) for x in source] + gather_scratch
    solve_scratch = [
        pltpu.VMEM(big, F32),
        pltpu.VMEM((VARS * SLOTS, LANES), F32),
        pltpu.VMEM((VARS * SLOTS, LANES), F32),
        pltpu.VMEM((2 * VARS * HALF, 256), F32),
        alike(visc),
        alike(forcing),
        dma((2,)),
    ]
    interp, state = call(
        first_kernel,
        "first",
        [shape(256, LANES), shape(*big)],
        (src_block, src_point, state, weight),
        source_scratch + [dma((4,))],
        outside=range(4),
    )
    got = exchange(interp, ("sweep", "grp"), 128)
    place, count, wide, factors, maps, dst_point, block_order = call(
        base_kernel,
        "base",
        [
            shape(256, SLOTS * LANES, dtype=BF16),
            shape(ROWS, LANES),
            shape(BLK, 3 * SQUARE, LANES),
            shape(3 * BLK, TILES, LANES),
            shape(FULL - BARE, TILES, LANES),
            alike(dst_point),
            alike(block_order),
        ],
        (dst_block, dst_point, diag, lowc, upc, inv, low_jac, up_jac, block_order),
        [alike(x) for x in (dst_block, diag, lowc, upc, inv, low_jac, up_jac)]
        + [
            pltpu.VMEM((HALF, SLOTS * LANES), BF16),
            pltpu.VMEM((3, VARS, BLK, VARS), F32),
            pltpu.VMEM((3 * BLK, VARS, VARS), F32),
            pltpu.VMEM((3 * SQUARE * BLK, LANES), F32),
            pltpu.VMEM((8, LANES), F32),
            dma((9,)),
        ],
        outside=range(9),
        beside=True,
    )

    def solve(full, got, state):
        operands = (got, dst_point, place, wide, factors, block_order, count, state, visc, forcing)
        operands += (maps,) if full else ()
        rows = FULL if full else BARE
        outs = [shape(TILES * rows, LANES), shape(BLK, VARS, TILES, LANES)]
        return call(lambda *refs: solve_kernel(full, *refs), "solve", outs, operands, solve_scratch, outside=(8, 9))

    def chain(values, coefs):
        rows = values.shape[0] // TILES
        outs = [shape(TILES * BARE, LANES)]
        return call(lambda *refs: chain_kernel(rows, *refs), "chain", outs, (values, coefs), chain_scratch)[0]

    chunk, z = solve(True, got, state)
    coefs = exchange(chunk, "sweep", TILES)
    back = exchange(chain(coefs, coefs), "sweep", TILES)
    state, interp = call(
        middle_kernel,
        "middle",
        [shape(*big), shape(256, LANES)],
        (back, z, state, wide, factors, block_order) + source,
        star_scratch + source_scratch + [dma((3,))],
        outside=(6, 7, 8),
    )
    got = exchange(interp, ("sweep", "grp"), 128)
    chunk, z = solve(False, got, state)
    back = exchange(chain(exchange(chunk, "sweep", TILES), coefs), "sweep", TILES)
    state, correction = call(
        finish, "finish", [jax.ShapeDtypeStruct(big, F32)] * 2, (back, z, state, wide, factors, block_order), star_scratch
    )
    return from_rows(state)[None], from_rows(correction)[None]


def solution(mesh):
    blocks = P("grp", "sweep", None, None)
    field = P("grp", "sweep", None)
    table = P(("sweep", "grp"), None, None)
    return jax.shard_map(
        per_device,
        mesh=mesh,
        in_specs=(
            blocks, blocks, field, blocks, blocks, blocks, field, field, field,
            table, table, P(("sweep", "grp"), None, None, None), table, table, P("grp", "sweep"),
        ),
        out_specs=(blocks, blocks),
        check_vma=False,
    )
```

time: 119 us -> 105 us (0.88)
  blocking collectives: 86.6 us -> 62.7 us
  starting transfers between devices: 0 us -> 11.5 us
  waiting for transfers between devices: 0 us -> 7.39 us
  local copies, waits for them, and re-layouts: 6.1 us -> 0 us
  Pallas kernels: 24.4 us -> 21.8 us
    all_to_all x6 -> x5, blocking collectives: 86.6 us -> 62.7 us  [exchange(): lax.all_to_all(parts, axes, split_axis=0, concat_axis=0, tiled=True)]
    all_to_all x0 -> x1, starting transfers between devices: none -> 11.5 us  [exchange(): lax.all_to_all(parts, axes, split_axis=0, concat_axis=0, tiled=True)]
    all_to_all x0 -> x1, waiting for transfers between devices: none -> 7.39 us  [exchange(): lax.all_to_all(parts, axes, split_axis=0, concat_axis=0, tiled=True)]
    unnamed x34 -> x0, local copies, waits for them, and re-layouts: 6.1 us -> none
    pallas_call x7 -> x8, Pallas kernels: 24.4 us -> 21.8 us  [call(): pl.pallas_call(kernel, out_shape=outs, in_specs=[pl.BlockSpec(memory_spac...]
  transfers between devices with their start and end apart: 0 -> 1, of which waited for: 0 -> 1; matrix products, arithmetic and copies ran while one was open for 0% -> 0% of each run, Pallas kernels for 0% -> 2%
where the time goes in v2:
time: 105 us; the launch traced here: 104 us
  blocking collectives  62.7 us (60%)
  Pallas kernels  21.8 us (21%)
  starting transfers between devices  11.5 us (11%)
  waiting for transfers between devices  7.39 us (7%)
    all_to_all x5, blocking collectives, exchange(): lax.all_to_all(parts, axes, split_axis=0, concat_axis=0, tiled=True)  62.7 us
    pallas_call x8, Pallas kernels, call(): pl.pallas_call(kernel, out_shape=outs, in_specs=[pl.BlockSpec(memory_spac...  21.8 us
    all_to_all x1, starting transfers between devices, exchange(): lax.all_to_all(parts, axes, split_axis=0, concat_axis=0, tiled=True)  11.5 us
    all_to_all x1, waiting for transfers between devices, exchange(): lax.all_to_all(parts, axes, split_axis=0, concat_axis=0, tiled=True)  7.39 us
  transfers between devices with their start and end apart: 1, of which 1 were waited for; matrix products, arithmetic and copies ran while one was open for 0% of the time, Pallas kernels for 2%

profile of v2, /device:TPU:1, one launch (start us, length us, event | category | flops | bytes accessed | tf_op | source)
XLA Modules:
  0.0 104.1 jit_solution(17345761096550744898)
XLA Ops:
  0.6 4.3 %first.1 = (f32[256,128]{1,0:T(8,128)}, f32[6,128,128]{2,1,0:T(8,128)S(1)}) custom-call(s32[32,128]{1,0:T(8,128)} %bitcast.96, s32[32,128]{1,0:T(8,128)} %bitcast.98, f32[6,128,128]{2,1,0:T(8,128)} %bitcast.91, f32[32,4,128]{2,1,0:T(4,128)} %bitcast.94), custom_call_target="tpu_custom_call" | custom-call | tf_op jit(solution)/shard_map/first/pallas_call | solution.py:400
  5.0 11.5 %all-to-all-start = ((f32[128,1,256]{2,1,0:T(1,128)}), f32[128,1,256]{2,1,0:T(1,128)S(1)}, u32[]{:S(2)}, u32[]{:S(2)}) async-start(f32[128,1,256]{2,1,0:T(1,128)} %bitcast.9), calls=%async_computation | async-start | bytes 262144 | tf_op jit(solution)/shard_map/all_to_all | solution.py:414
  16.5 2.4 %base.1 = (bf16[256,4096]{1,0:T(8,128)(2,1)S(1)}, f32[128,128]{1,0:T(8,128)S(1)}, f32[4,108,128]{2,1,0:T(8,128)S(1)}, f32[12,32,128]{2,1,0:T(8,128)S(1)}, f32[8,...) custom-call(s32[32,128]{1,0:T(8,128)} %bitcast.105, s32[32,128]{1,0:T(8,128)} %bitcast.106, ...), custom_call_target="tpu_custom_call" | custom-call | flops 20000000000 | bytes 4000000 | tf_op jit(solution)/shard_map/base/pallas_call | solution.py:400
  18.9 7.4 %all-to-all-done = f32[128,1,256]{2,1,0:T(1,128)S(1)} async-done(((f32[128,1,256]{2,1,0:T(1,128)}), f32[128,1,256]{2,1,0:T(1,128)S(1)}, u32[]{:S(2)}, u32[]{:S(2)}) %all-to-all-start) | async-done | bytes 131104 | tf_op jit(solution)/shard_map/all_to_all | solution.py:414
  26.3 3.1 %solve.2 = (f32[640,128]{1,0:T(8,128)S(1)}, f32[4,6,32,128]{3,2,1,0:T(8,128)S(1)}) custom-call(f32[256,128]{1,0:T(8,128)S(1)} %bitcast.84, s32[32,128]{1,0:T(8,128)S(1)} %get-tuple-element.20.refs_1_, bf16[256,4096]{1,0:T(8,128)(2,1)S(1)} %get-tuple-element.21.refs_2_, f32[4,108,128]{2,1,0:T(8,128)S(1)} %get-tuple-element.22.refs_3_.wide_ref, ...), custom_call_target="tpu_custom_call" | custom-call | tf_op jit(solution)/shard_map/solve/pallas_call | solution.py:400
  29.5 13.3 %all_to_all.30 = f32[32,1,2560]{2,1,0:T(1,128)S(1)} all-to-all(f32[32,1,2560]{2,1,0:T(1,128)S(1)} %bitcast.86), channel_id=1, replica_groups=mesh['sweep'=32,'grp'=4] {'sweep'}, dimensions={0} | all-to-all | bytes 655360 | tf_op jit(solution)/shard_map/all_to_all | solution.py:414
  42.7 2.2 %chain.2 = f32[384,128]{1,0:T(8,128)S(1)} custom-call(f32[640,128]{1,0:T(8,128)S(1)} %bitcast.76, f32[640,128]{1,0:T(8,128)S(1)} %bitcast.77), custom_call_target="tpu_custom_call" | custom-call | tf_op jit(solution)/shard_map/chain/pallas_call | solution.py:400
  44.9 11.8 %all_to_all.31 = f32[32,1,1536]{2,1,0:T(1,128)S(1)} all-to-all(f32[32,1,1536]{2,1,0:T(1,128)S(1)} %bitcast.83), channel_id=1, replica_groups=mesh['sweep'=32,'grp'=4] {'sweep'}, dimensions={0} | all-to-all | bytes 393216 | tf_op jit(solution)/shard_map/all_to_all | solution.py:414
  56.8 3.5 %middle.1 = (f32[6,128,128]{2,1,0:T(8,128)S(1)}, f32[256,128]{1,0:T(8,128)S(1)}) custom-call(f32[384,128]{1,0:T(8,128)S(1)} %bitcast.82, f32[4,6,32,128]{3,2,1,0:T(8,128)S(1)} %get-tuple-element.29.z_ref, f32[6,128,128]{2,1,0:T(8,128)S(1)} %get-tuple-element.26.refs_7_.state_ref, f32[4,108,128]{2,1,0:T(8,128)S(1)} %get-tuple-element.22.refs_3_.wide_ref, ...), custom_call_target="tpu_custom_call" | custom-call | tf_op jit(solution)/shard_map/middle/pallas_call | solution.py:400
  60.3 14.1 %all_to_all.32 = f32[128,1,256]{2,1,0:T(1,128)S(1)} all-to-all(f32[128,1,256]{2,1,0:T(1,128)S(1)} %bitcast.88), channel_id=1, replica_groups=mesh['sweep'=32,'grp'=4] {'sweep','grp'}, dimensions={0} | all-to-all | bytes 262144 | tf_op jit(solution)/shard_map/all_to_all | solution.py:414
  74.4 2.7 %solve.3 = (f32[384,128]{1,0:T(8,128)S(1)}, f32[4,6,32,128]{3,2,1,0:T(8,128)S(1)}) custom-call(f32[256,128]{1,0:T(8,128)S(1)} %bitcast.85, s32[32,128]{1,0:T(8,128)S(1)} %get-tuple-element.20.refs_1_, bf16[256,4096]{1,0:T(8,128)(2,1)S(1)} %get-tuple-element.21.refs_2_, f32[4,108,128]{2,1,0:T(8,128)S(1)} %get-tuple-element.22.refs_3_.wide_ref, ...), custom_call_target="tpu_custom_call" | custom-call | tf_op jit(solution)/shard_map/solve/pallas_call | solution.py:400
  77.1 11.7 %all_to_all.33 = f32[32,1,1536]{2,1,0:T(1,128)S(1)} all-to-all(f32[32,1,1536]{2,1,0:T(1,128)S(1)} %bitcast.87), channel_id=1, replica_groups=mesh['sweep'=32,'grp'=4] {'sweep'}, dimensions={0} | all-to-all | bytes 393216 | tf_op jit(solution)/shard_map/all_to_all | solution.py:414
  88.7 2.2 %chain.3 = f32[384,128]{1,0:T(8,128)S(1)} custom-call(f32[384,128]{1,0:T(8,128)S(1)} %bitcast.80, f32[640,128]{1,0:T(8,128)S(1)} %bitcast.78), custom_call_target="tpu_custom_call" | custom-call | tf_op jit(solution)/shard_map/chain/pallas_call | solution.py:400
  90.9 11.9 %all_to_all.34 = f32[32,1,1536]{2,1,0:T(1,128)S(1)} all-to-all(f32[32,1,1536]{2,1,0:T(1,128)S(1)} %bitcast.81), channel_id=1, replica_groups=mesh['sweep'=32,'grp'=4] {'sweep'}, dimensions={0} | all-to-all | bytes 393216 | tf_op jit(solution)/shard_map/all_to_all | solution.py:414
  102.8 1.3 %finish.1 = (f32[6,128,128]{2,1,0:T(8,128)}, f32[6,128,128]{2,1,0:T(8,128)}) custom-call(f32[384,128]{1,0:T(8,128)S(1)} %bitcast.79, f32[4,6,32,128]{3,2,1,0:T(8,128)S(1)} %get-tuple-element.33.z_ref, f32[6,128,128]{2,1,0:T(8,128)S(1)} %get-tuple-element.31.refs_7_.state_ref, f32[4,108,128]{2,1,0:T(8,128)S(1)} %get-tuple-element.22.refs_3_.wide_ref, ...), custom_call_target="tpu_custom_call" | custom-call | tf_op jit(solution)/shard_map/finish/pallas_call | solution.py:400
Async XLA Ops:
  5.0 21.4 %all-to-all-start = ((f32[128,1,256]{2,1,0:T(1,128)}), f32[128,1,256]{2,1,0:T(1,128)S(1)}, u32[]{:S(2)}, u32[]{:S(2)}) async-start(f32[128,1,256]{2,1,0:T(1,128)} %bitcast.9), calls=%async_computation | async-start | bytes 262144 | tf_op jit(solution)/shard_map/all_to_all | solution.py:414

commit v3 on v2

--- a/solution.py
+++ b/solution.py
@@ -41,8 +41,10 @@
 
 
 def one_hot(count, index):
-    places = lax.broadcasted_iota(jnp.int32, (count, index.shape[1]), 0)
-    return jnp.where(places == index, 1.0, 0.0).astype(BF16)
+    size = (count, index.shape[1])
+    places = lax.broadcasted_iota(jnp.int32, size, 0).astype(F32).astype(BF16)
+    index = jnp.broadcast_to(index.astype(F32), size).astype(BF16)
+    return jnp.where(places == index, jnp.ones((), BF16), jnp.zeros((), BF16))
 
 
 def window_of(block, point):
@@ -81,13 +83,16 @@
     return row
 
 
-def gather(block_ref, point_ref, weight_ref, out_ref, high_ref, low_ref, acc_ref):
+def picks(block_ref, point_ref, pick_ref):
+    for c in range(SLOTS):
+        window = window_of(block_ref[c : c + 1], point_ref[c : c + 1])
+        pick_ref[:, c * LANES : (c + 1) * LANES] = one_hot(256, window)
+
+
+def gather(pick_ref, point_ref, weight_ref, out_ref, high_ref, low_ref, acc_ref):
     acc_ref[VARS * SLOTS :] = jnp.zeros((256 - VARS * SLOTS, LANES), F32)
     for first in range(0, SLOTS, GROUP):
-        picks = []
-        for c in range(first, first + GROUP):
-            picks.append(one_hot(256, window_of(block_ref[c : c + 1], point_ref[c : c + 1])))
-        pick = jnp.concatenate(picks, axis=1)
+        pick = pick_ref[:, first * LANES : (first + GROUP) * LANES]
         found = jnp.dot(high_ref[...], pick, preferred_element_type=F32)
         found = found + jnp.dot(low_ref[...], pick, preferred_element_type=F32)
         for n in range(GROUP):
@@ -111,13 +116,18 @@
 
 
 def first_kernel(
-    block_hbm, point_hbm, state_hbm, weight_hbm, out_ref, state_ref, block_s, point_s, weight_s, high_s, low_s, acc_s, sems
+    block_hbm, point_hbm, state_hbm, weight_hbm, out_ref, state_ref,
+    block_s, point_s, weight_s, pick_s, high_s, low_s, acc_s, sems,
 ):
     pairs = ((block_hbm, block_s), (point_hbm, point_s), (state_hbm, state_ref), (weight_hbm, weight_s))
-    for copy in fetch(pairs, sems):
-        copy.wait()
+    copies = fetch(pairs, sems)
+    copies[0].wait()
+    copies[1].wait()
+    picks(block_s, point_s, pick_s)
+    copies[2].wait()
     windows(state_ref, high_s, low_s)
-    gather(block_s, point_s, weight_s, out_ref, high_s, low_s, acc_s)
+    copies[3].wait()
+    gather(pick_s, point_s, weight_s, out_ref, high_s, low_s, acc_s)
 
 
 def product(a, b):
@@ -310,7 +320,31 @@
             put(VARS + i, y[i])
 
 
-def chain_kernel(rows, in_ref, coef_ref, out_ref, value_s, mid_s, mats_s):
+MATS = 6
+
+
+def columns(mats, cols_ref):
+    lane = lax.broadcasted_iota(jnp.int32, mats.shape, 1)
+    mats = jnp.where(lane < SQUARE, mats, 0.0)
+    packed = mats.astype(BF16).astype(F32)
+    rest = mats - packed
+    for n in (1, 2):
+        part = rest.astype(BF16).astype(F32)
+        rest = rest - part
+        packed = packed + pltpu.roll(part, n * SQUARE, 1)
+    packed = packed.astype(BF16)
+    row = lax.broadcasted_iota(jnp.int32, (LANES, LANES), 0)
+    row = row - jnp.where(row >= SQUARE, SQUARE, 0) - jnp.where(row >= 2 * SQUARE, SQUARE, 0)
+    row = row.astype(F32).astype(BF16)
+    for m in range(MATS):
+        copies = [
+            jnp.where(row == jnp.asarray(m * VARS + j, BF16), jnp.ones((), BF16), jnp.zeros((), BF16)) for j in range(VARS)
+        ]
+        spread = jnp.dot(packed, jnp.concatenate(copies, axis=1), preferred_element_type=F32)
+        cols_ref[:, m * VARS * LANES : (m + 1) * VARS * LANES] = spread
+
+
+def chain_kernel(rows, in_ref, coef_ref, out_ref, value_s, mid_s, mats_s, cols_s):
     for half in range(2):
         lines = coef_ref[pl.ds(FULL - 2 + half, TILES, stride=FULL), :]
         for n in range(3):
@@ -320,12 +354,15 @@
             to = value_s if half == 0 else mid_s
             to[pl.ds(i, TILES, stride=8), :] = in_ref[pl.ds(half * VARS + i, TILES, stride=rows), :]
 
-    def apply(mats, m, x):
+    for i in (VARS, VARS + 1):
+        mats_s[pl.ds(i, TILES, stride=8), :] = jnp.zeros((TILES, LANES), F32)
+    columns(mats_s[...], cols_s)
+
+    def apply(here, m, x):
         terms = []
         for j in range(VARS):
-            at = m * VARS + j
-            column = jnp.broadcast_to(mats[:, at : at + 1], (VARS, LANES))
-            terms.append(column * x[j])
+            at = (m * VARS + j) * LANES
+            terms.append(cols_s[here, at : at + LANES] * x[j])
         return ((terms[0] + terms[1]) + (terms[2] + terms[3])) + (terms[4] + terms[5])
 
     def spread(x):
@@ -337,19 +374,18 @@
     down = jnp.zeros((VARS, LANES), F32)
     for s in range(TILES):
         here = slice(8 * s, 8 * s + VARS)
-        mats = mats_s[here]
         parts = spread(down)
         mid = mid_s[here]
         for k in range(BLK):
-            mid = mid + coef(s, 2 + k) * apply(mats, 2 + k, parts)
+            mid = mid + coef(s, 2 + k) * apply(here, 2 + k, parts)
         mid_s[here] = mid
-        after = coef(s, 0) * apply(mats, 0, parts) + value_s[here]
+        after = coef(s, 0) * apply(here, 0, parts) + value_s[here]
         value_s[here] = down
         down = after
     up = jnp.zeros((VARS, LANES), F32)
     for s in reversed(range(TILES)):
         here = slice(8 * s, 8 * s + VARS)
-        after = coef(s, 1) * apply(mats_s[here], 1, spread(up)) + mid_s[here]
+        after = coef(s, 1) * apply(here, 1, spread(up)) + mid_s[here]
         mid_s[here] = up
         up = after
     for i in range(VARS):
@@ -381,14 +417,15 @@
 
 def middle_kernel(
     back_ref, z_ref, state_ref, wide_ref, factor_ref, order_ref, block_hbm, point_hbm, weight_hbm, new_ref, out_ref,
-    star_s, block_s, point_s, weight_s, high_s, low_s, acc_s, sems,
+    star_s, block_s, point_s, weight_s, pick_s, high_s, low_s, acc_s, sems,
 ):
     copies = fetch(((block_hbm, block_s), (point_hbm, point_s), (weight_hbm, weight_s)), sems)
     finish(back_ref, z_ref, state_ref, wide_ref, factor_ref, order_ref, new_ref, None, star_s)
     windows(new_ref, high_s, low_s)
     for copy in copies:
         copy.wait()
-    gather(block_s, point_s, weight_s, out_ref, high_s, low_s, acc_s)
+    picks(block_s, point_s, pick_s)
+    gather(pick_s, point_s, weight_s, out_ref, high_s, low_s, acc_s)
 
 
 def shape(*dims, dtype=F32):
@@ -428,13 +465,14 @@
     gather_scratch = [pltpu.VMEM((sent, 256), BF16), pltpu.VMEM((sent, 256), BF16), pltpu.VMEM((256, LANES), F32)]
     star_scratch = [pltpu.VMEM((BLK, VARS, TILES, LANES), F32)]
     chain_scratch = [pltpu.VMEM((TILES * 8, LANES), F32) for _ in range(3)]
+    chain_scratch += [pltpu.VMEM((TILES * 8, MATS * VARS * LANES), F32)]
     dma = pltpu.SemaphoreType.DMA
 
     def alike(x):
         return pltpu.VMEM(x.shape, x.dtype)
 
     source = (src_block, src_point, weight)
-    source_scratch = [alike(x) for x in source] + gather_scratch
+    source_scratch = [alike(x) for x in source] + [pltpu.VMEM((256, SLOTS * LANES), BF16)] + gather_scratch
     solve_scratch = [
         pltpu.VMEM(big, F32),
         pltpu.VMEM((VARS * SLOTS, LANES), F32),

time: 105 us -> 103 us (0.981)
  Pallas kernels: 21.8 us -> 19.7 us
    pallas_call x8, Pallas kernels: 21.8 us -> 19.7 us  [call(): pl.pallas_call(kernel, out_shape=outs, in_specs=[pl.BlockSpec(memory_spac...]
where the time goes in v3:
time: 103 us; the launch traced here: 102 us
  blocking collectives  62.7 us (61%)
  Pallas kernels  19.7 us (19%)
  starting transfers between devices  11.5 us (11%)
  waiting for transfers between devices  7.63 us (7%)
    all_to_all x5, blocking collectives, exchange(): lax.all_to_all(parts, axes, split_axis=0, concat_axis=0, tiled=True)  62.7 us
    pallas_call x8, Pallas kernels, call(): pl.pallas_call(kernel, out_shape=outs, in_specs=[pl.BlockSpec(memory_spac...  19.7 us
    all_to_all x1, starting transfers between devices, exchange(): lax.all_to_all(parts, axes, split_axis=0, concat_axis=0, tiled=True)  11.5 us
    all_to_all x1, waiting for transfers between devices, exchange(): lax.all_to_all(parts, axes, split_axis=0, concat_axis=0, tiled=True)  7.63 us
  transfers between devices with their start and end apart: 1, of which 1 were waited for; matrix products, arithmetic and copies ran while one was open for 0% of the time, Pallas kernels for 2%

profile of v3, /device:TPU:1, one launch (start us, length us, event | category | flops | bytes accessed | tf_op | source)
XLA Modules:
  0.0 102.3 jit_solution(13432400075737155978)
XLA Ops:
  0.6 4.3 %first.1 = (f32[256,128]{1,0:T(8,128)}, f32[6,128,128]{2,1,0:T(8,128)S(1)}) custom-call(s32[32,128]{1,0:T(8,128)} %bitcast.96, s32[32,128]{1,0:T(8,128)} %bitcast.98, f32[6,128,128]{2,1,0:T(8,128)} %bitcast.91, f32[32,4,128]{2,1,0:T(4,128)} %bitcast.94), custom_call_target="tpu_custom_call" | custom-call | tf_op jit(solution)/shard_map/first/pallas_call | solution.py:437
  5.0 11.5 %all-to-all-start = ((f32[128,1,256]{2,1,0:T(1,128)}), f32[128,1,256]{2,1,0:T(1,128)S(1)}, u32[]{:S(2)}, u32[]{:S(2)}) async-start(f32[128,1,256]{2,1,0:T(1,128)} %bitcast.9), calls=%async_computation | async-start | bytes 262144 | tf_op jit(solution)/shard_map/all_to_all | solution.py:451
  16.5 2.2 %base.1 = (bf16[256,4096]{1,0:T(8,128)(2,1)S(1)}, f32[128,128]{1,0:T(8,128)S(1)}, f32[4,108,128]{2,1,0:T(8,128)S(1)}, f32[12,32,128]{2,1,0:T(8,128)S(1)}, f32[8,...) custom-call(s32[32,128]{1,0:T(8,128)} %bitcast.105, s32[32,128]{1,0:T(8,128)} %bitcast.106, ...), custom_call_target="tpu_custom_call" | custom-call | flops 20000000000 | bytes 4000000 | tf_op jit(solution)/shard_map/base/pallas_call | solution.py:437
  18.7 7.6 %all-to-all-done = f32[128,1,256]{2,1,0:T(1,128)S(1)} async-done(((f32[128,1,256]{2,1,0:T(1,128)}), f32[128,1,256]{2,1,0:T(1,128)S(1)}, u32[]{:S(2)}, u32[]{:S(2)}) %all-to-all-start) | async-done | bytes 131104 | tf_op jit(solution)/shard_map/all_to_all | solution.py:451
  26.3 3.1 %solve.2 = (f32[640,128]{1,0:T(8,128)S(1)}, f32[4,6,32,128]{3,2,1,0:T(8,128)S(1)}) custom-call(f32[256,128]{1,0:T(8,128)S(1)} %bitcast.84, s32[32,128]{1,0:T(8,128)S(1)} %get-tuple-element.20.refs_1_, bf16[256,4096]{1,0:T(8,128)(2,1)S(1)} %get-tuple-element.21.refs_2_, f32[4,108,128]{2,1,0:T(8,128)S(1)} %get-tuple-element.22.refs_3_.wide_ref, ...), custom_call_target="tpu_custom_call" | custom-call | tf_op jit(solution)/shard_map/solve/pallas_call | solution.py:437
  29.4 13.3 %all_to_all.30 = f32[32,1,2560]{2,1,0:T(1,128)S(1)} all-to-all(f32[32,1,2560]{2,1,0:T(1,128)S(1)} %bitcast.86), channel_id=1, replica_groups=mesh['sweep'=32,'grp'=4] {'sweep'}, dimensions={0} | all-to-all | bytes 655360 | tf_op jit(solution)/shard_map/all_to_all | solution.py:451
  42.7 1.4 %chain.2 = f32[384,128]{1,0:T(8,128)S(1)} custom-call(f32[640,128]{1,0:T(8,128)S(1)} %bitcast.76, f32[640,128]{1,0:T(8,128)S(1)} %bitcast.77), custom_call_target="tpu_custom_call" | custom-call | tf_op jit(solution)/shard_map/chain/pallas_call | solution.py:437
  44.1 11.8 %all_to_all.31 = f32[32,1,1536]{2,1,0:T(1,128)S(1)} all-to-all(f32[32,1,1536]{2,1,0:T(1,128)S(1)} %bitcast.83), channel_id=1, replica_groups=mesh['sweep'=32,'grp'=4] {'sweep'}, dimensions={0} | all-to-all | bytes 393216 | tf_op jit(solution)/shard_map/all_to_all | solution.py:451
  55.9 3.4 %middle.1 = (f32[6,128,128]{2,1,0:T(8,128)S(1)}, f32[256,128]{1,0:T(8,128)S(1)}) custom-call(f32[384,128]{1,0:T(8,128)S(1)} %bitcast.82, f32[4,6,32,128]{3,2,1,0:T(8,128)S(1)} %get-tuple-element.29.z_ref, f32[6,128,128]{2,1,0:T(8,128)S(1)} %get-tuple-element.26.refs_7_.state_ref, f32[4,108,128]{2,1,0:T(8,128)S(1)} %get-tuple-element.22.refs_3_.wide_ref, ...), custom_call_target="tpu_custom_call" | custom-call | tf_op jit(solution)/shard_map/middle/pallas_call | solution.py:437
  59.3 14.1 %all_to_all.32 = f32[128,1,256]{2,1,0:T(1,128)S(1)} all-to-all(f32[128,1,256]{2,1,0:T(1,128)S(1)} %bitcast.88), channel_id=1, replica_groups=mesh['sweep'=32,'grp'=4] {'sweep','grp'}, dimensions={0} | all-to-all | bytes 262144 | tf_op jit(solution)/shard_map/all_to_all | solution.py:451
  73.4 2.7 %solve.3 = (f32[384,128]{1,0:T(8,128)S(1)}, f32[4,6,32,128]{3,2,1,0:T(8,128)S(1)}) custom-call(f32[256,128]{1,0:T(8,128)S(1)} %bitcast.85, s32[32,128]{1,0:T(8,128)S(1)} %get-tuple-element.20.refs_1_, bf16[256,4096]{1,0:T(8,128)(2,1)S(1)} %get-tuple-element.21.refs_2_, f32[4,108,128]{2,1,0:T(8,128)S(1)} %get-tuple-element.22.refs_3_.wide_ref, ...), custom_call_target="tpu_custom_call" | custom-call | tf_op jit(solution)/shard_map/solve/pallas_call | solution.py:437
  76.1 11.6 %all_to_all.33 = f32[32,1,1536]{2,1,0:T(1,128)S(1)} all-to-all(f32[32,1,1536]{2,1,0:T(1,128)S(1)} %bitcast.87), channel_id=1, replica_groups=mesh['sweep'=32,'grp'=4] {'sweep'}, dimensions={0} | all-to-all | bytes 393216 | tf_op jit(solution)/shard_map/all_to_all | solution.py:451
  87.7 1.4 %chain.3 = f32[384,128]{1,0:T(8,128)S(1)} custom-call(f32[384,128]{1,0:T(8,128)S(1)} %bitcast.80, f32[640,128]{1,0:T(8,128)S(1)} %bitcast.78), custom_call_target="tpu_custom_call" | custom-call | tf_op jit(solution)/shard_map/chain/pallas_call | solution.py:437
  89.1 11.9 %all_to_all.34 = f32[32,1,1536]{2,1,0:T(1,128)S(1)} all-to-all(f32[32,1,1536]{2,1,0:T(1,128)S(1)} %bitcast.81), channel_id=1, replica_groups=mesh['sweep'=32,'grp'=4] {'sweep'}, dimensions={0} | all-to-all | bytes 393216 | tf_op jit(solution)/shard_map/all_to_all | solution.py:451
  101.0 1.3 %finish.1 = (f32[6,128,128]{2,1,0:T(8,128)}, f32[6,128,128]{2,1,0:T(8,128)}) custom-call(f32[384,128]{1,0:T(8,128)S(1)} %bitcast.79, f32[4,6,32,128]{3,2,1,0:T(8,128)S(1)} %get-tuple-element.33.z_ref, f32[6,128,128]{2,1,0:T(8,128)S(1)} %get-tuple-element.31.refs_7_.state_ref, f32[4,108,128]{2,1,0:T(8,128)S(1)} %get-tuple-element.22.refs_3_.wide_ref, ...), custom_call_target="tpu_custom_call" | custom-call | tf_op jit(solution)/shard_map/finish/pallas_call | solution.py:437
Async XLA Ops:
  5.0 21.4 %all-to-all-start = ((f32[128,1,256]{2,1,0:T(1,128)}), f32[128,1,256]{2,1,0:T(1,128)S(1)}, u32[]{:S(2)}, u32[]{:S(2)}) async-start(f32[128,1,256]{2,1,0:T(1,128)} %bitcast.9), calls=%async_computation | async-start | bytes 262144 | tf_op jit(solution)/shard_map/all_to_all | solution.py:451

commit v4 on v3

--- a/solution.py
+++ b/solution.py
@@ -344,25 +344,32 @@
         cols_ref[:, m * VARS * LANES : (m + 1) * VARS * LANES] = spread
 
 
-def chain_kernel(rows, in_ref, coef_ref, out_ref, value_s, mid_s, mats_s, cols_s):
+def first_chain_kernel(coef_ref, out_ref, cols_ref, value_s, mid_s, mats_s):
     for half in range(2):
         lines = coef_ref[pl.ds(FULL - 2 + half, TILES, stride=FULL), :]
         for n in range(3):
             shifted = pltpu.roll(lines, LANES - n * SQUARE, 1) if n else lines
             mats_s[pl.ds(3 * half + n, TILES, stride=8), :] = shifted
-        for i in range(VARS):
-            to = value_s if half == 0 else mid_s
-            to[pl.ds(i, TILES, stride=8), :] = in_ref[pl.ds(half * VARS + i, TILES, stride=rows), :]
-
     for i in (VARS, VARS + 1):
         mats_s[pl.ds(i, TILES, stride=8), :] = jnp.zeros((TILES, LANES), F32)
-    columns(mats_s[...], cols_s)
+    columns(mats_s[...], cols_ref)
+    chain(FULL, coef_ref, coef_ref, cols_ref, out_ref, value_s, mid_s)
+
+
+def second_chain_kernel(in_ref, coef_ref, cols_ref, out_ref, value_s, mid_s):
+    chain(BARE, in_ref, coef_ref, cols_ref, out_ref, value_s, mid_s)
+
+
+def chain(rows, in_ref, coef_ref, cols_ref, out_ref, value_s, mid_s):
+    for i in range(VARS):
+        value_s[pl.ds(i, TILES, stride=8), :] = in_ref[pl.ds(i, TILES, stride=rows), :]
+        mid_s[pl.ds(i, TILES, stride=8), :] = in_ref[pl.ds(VARS + i, TILES, stride=rows), :]
 
     def apply(here, m, x):
         terms = []
         for j in range(VARS):
             at = (m * VARS + j) * LANES
-            terms.append(cols_s[here, at : at + LANES] * x[j])
+            terms.append(cols_ref[here, at : at + LANES] * x[j])
         return ((terms[0] + terms[1]) + (terms[2] + terms[3])) + (terms[4] + terms[5])
 
     def spread(x):
@@ -465,7 +472,6 @@
     gather_scratch = [pltpu.VMEM((sent, 256), BF16), pltpu.VMEM((sent, 256), BF16), pltpu.VMEM((256, LANES), F32)]
     star_scratch = [pltpu.VMEM((BLK, VARS, TILES, LANES), F32)]
     chain_scratch = [pltpu.VMEM((TILES * 8, LANES), F32) for _ in range(3)]
-    chain_scratch += [pltpu.VMEM((TILES * 8, MATS * VARS * LANES), F32)]
     dma = pltpu.SemaphoreType.DMA
 
     def alike(x):
@@ -524,14 +530,16 @@
         outs = [shape(TILES * rows, LANES), shape(BLK, VARS, TILES, LANES)]
         return call(lambda *refs: solve_kernel(full, *refs), "solve", outs, operands, solve_scratch, outside=(8, 9))
 
-    def chain(values, coefs):
-        rows = values.shape[0] // TILES
-        outs = [shape(TILES * BARE, LANES)]
-        return call(lambda *refs: chain_kernel(rows, *refs), "chain", outs, (values, coefs), chain_scratch)[0]
-
     chunk, z = solve(True, got, state)
     coefs = exchange(chunk, "sweep", TILES)
-    back = exchange(chain(coefs, coefs), "sweep", TILES)
+    entering, cols = call(
+        first_chain_kernel,
+        "chain",
+        [shape(TILES * BARE, LANES), shape(TILES * 8, MATS * VARS * LANES)],
+        (coefs,),
+        chain_scratch,
+    )
+    back = exchange(entering, "sweep", TILES)
     state, interp = call(
         middle_kernel,
         "middle",
@@ -542,7 +550,11 @@
     )
     got = exchange(interp, ("sweep", "grp"), 128)
     chunk, z = solve(False, got, state)
-    back = exchange(chain(exchange(chunk, "sweep", TILES), coefs), "sweep", TILES)
+    values = exchange(chunk, "sweep", TILES)
+    (entering,) = call(
+        second_chain_kernel, "chain", [shape(TILES * BARE, LANES)], (values, coefs, cols), chain_scratch[:2]
+    )
+    back = exchange(entering, "sweep", TILES)
     state, correction = call(
         finish, "finish", [jax.ShapeDtypeStruct(big, F32)] * 2, (back, z, state, wide, factors, block_order), star_scratch
     )

time: 103 us -> 102 us (level)
  no operation moved by 1% of the time
where the time goes in v4:
time: 102 us
  blocking collectives  62.7 us (61%)
  Pallas kernels  19.1 us (19%)
  starting transfers between devices  11.5 us (11%)
  waiting for transfers between devices  7.63 us (7%)
    all_to_all x5, blocking collectives, exchange(): lax.all_to_all(parts, axes, split_axis=0, concat_axis=0, tiled=True)  62.7 us
    pallas_call x8, Pallas kernels, call(): pl.pallas_call(kernel, out_shape=outs, in_specs=[pl.BlockSpec(memory_spac...  19.1 us
    all_to_all x1, starting transfers between devices, exchange(): lax.all_to_all(parts, axes, split_axis=0, concat_axis=0, tiled=True)  11.5 us
    all_to_all x1, waiting for transfers between devices, exchange(): lax.all_to_all(parts, axes, split_axis=0, concat_axis=0, tiled=True)  7.63 us
  transfers between devices with their start and end apart: 1, of which 1 were waited for; matrix products, arithmetic and copies ran while one was open for 0% of the time, Pallas kernels for 2%

profile of v4, /device:TPU:1, one launch (start us, length us, event | category | flops | bytes accessed | tf_op | source)
XLA Modules:
  0.0 101.6 jit_solution(2268359652524956162)
XLA Ops:
  0.6 4.3 %first.1 = (f32[256,128]{1,0:T(8,128)}, f32[6,128,128]{2,1,0:T(8,128)S(1)}) custom-call(s32[32,128]{1,0:T(8,128)} %bitcast.95, s32[32,128]{1,0:T(8,128)} %bitcast.97, f32[6,128,128]{2,1,0:T(8,128)} %bitcast.90, f32[32,4,128]{2,1,0:T(4,128)} %bitcast.93), custom_call_target="tpu_custom_call" | custom-call | tf_op jit(solution)/shard_map/first/pallas_call | solution.py:444
  5.0 11.5 %all-to-all-start = ((f32[128,1,256]{2,1,0:T(1,128)}), f32[128,1,256]{2,1,0:T(1,128)S(1)}, u32[]{:S(2)}, u32[]{:S(2)}) async-start(f32[128,1,256]{2,1,0:T(1,128)} %bitcast.9), calls=%async_computation | async-start | bytes 262144 | tf_op jit(solution)/shard_map/all_to_all | solution.py:458
  16.5 2.2 %base.1 = (bf16[256,4096]{1,0:T(8,128)(2,1)S(1)}, f32[128,128]{1,0:T(8,128)S(1)}, f32[4,108,128]{2,1,0:T(8,128)S(1)}, f32[12,32,128]{2,1,0:T(8,128)S(1)}, f32[8,...) custom-call(s32[32,128]{1,0:T(8,128)} %bitcast.104, s32[32,128]{1,0:T(8,128)} %bitcast.105, ...), custom_call_target="tpu_custom_call" | custom-call | flops 20000000000 | bytes 4000000 | tf_op jit(solution)/shard_map/base/pallas_call | solution.py:444
  18.7 7.6 %all-to-all-done = f32[128,1,256]{2,1,0:T(1,128)S(1)} async-done(((f32[128,1,256]{2,1,0:T(1,128)}), f32[128,1,256]{2,1,0:T(1,128)S(1)}, u32[]{:S(2)}, u32[]{:S(2)}) %all-to-all-start) | async-done | bytes 131104 | tf_op jit(solution)/shard_map/all_to_all | solution.py:458
  26.3 3.1 %solve.2 = (f32[640,128]{1,0:T(8,128)S(1)}, f32[4,6,32,128]{3,2,1,0:T(8,128)S(1)}) custom-call(f32[256,128]{1,0:T(8,128)S(1)} %bitcast.82, s32[32,128]{1,0:T(8,128)S(1)} %get-tuple-element.22.refs_1_, bf16[256,4096]{1,0:T(8,128)(2,1)S(1)} %get-tuple-element.23.refs_2_, f32[4,108,128]{2,1,0:T(8,128)S(1)} %get-tuple-element.24.refs_3_.wide_ref, ...), custom_call_target="tpu_custom_call" | custom-call | tf_op jit(solution)/shard_map/solve/pallas_call | solution.py:444
  29.4 13.3 %all_to_all.30 = f32[32,1,2560]{2,1,0:T(1,128)S(1)} all-to-all(f32[32,1,2560]{2,1,0:T(1,128)S(1)} %bitcast.84), channel_id=1, replica_groups=mesh['sweep'=32,'grp'=4] {'sweep'}, dimensions={0} | all-to-all | bytes 655360 | tf_op jit(solution)/shard_map/all_to_all | solution.py:458
  42.7 1.3 %chain.2 = (f32[384,128]{1,0:T(8,128)S(1)}, f32[256,4608]{1,0:T(8,128)S(1)}) custom-call(f32[640,128]{1,0:T(8,128)S(1)} %bitcast.76), custom_call_target="tpu_custom_call" | custom-call | tf_op jit(solution)/shard_map/chain/pallas_call | solution.py:444
  44.1 11.8 %all_to_all.31 = f32[32,1,1536]{2,1,0:T(1,128)S(1)} all-to-all(f32[32,1,1536]{2,1,0:T(1,128)S(1)} %bitcast.86), channel_id=1, replica_groups=mesh['sweep'=32,'grp'=4] {'sweep'}, dimensions={0} | all-to-all | bytes 393216 | tf_op jit(solution)/shard_map/all_to_all | solution.py:458
  55.9 3.4 %middle.1 = (f32[6,128,128]{2,1,0:T(8,128)S(1)}, f32[256,128]{1,0:T(8,128)S(1)}) custom-call(f32[384,128]{1,0:T(8,128)S(1)} %bitcast.79, f32[4,6,32,128]{3,2,1,0:T(8,128)S(1)} %get-tuple-element.32.z_ref, f32[6,128,128]{2,1,0:T(8,128)S(1)} %get-tuple-element.28.refs_7_.state_ref, f32[4,108,128]{2,1,0:T(8,128)S(1)} %get-tuple-element.24.refs_3_.wide_ref, ...), custom_call_target="tpu_custom_call" | custom-call | tf_op jit(solution)/shard_map/middle/pallas_call | solution.py:444
  59.3 14.1 %all_to_all.32 = f32[128,1,256]{2,1,0:T(1,128)S(1)} all-to-all(f32[128,1,256]{2,1,0:T(1,128)S(1)} %bitcast.87), channel_id=1, replica_groups=mesh['sweep'=32,'grp'=4] {'sweep','grp'}, dimensions={0} | all-to-all | bytes 262144 | tf_op jit(solution)/shard_map/all_to_all | solution.py:458
  73.4 2.7 %solve.3 = (f32[384,128]{1,0:T(8,128)S(1)}, f32[4,6,32,128]{3,2,1,0:T(8,128)S(1)}) custom-call(f32[256,128]{1,0:T(8,128)S(1)} %bitcast.83, s32[32,128]{1,0:T(8,128)S(1)} %get-tuple-element.22.refs_1_, bf16[256,4096]{1,0:T(8,128)(2,1)S(1)} %get-tuple-element.23.refs_2_, f32[4,108,128]{2,1,0:T(8,128)S(1)} %get-tuple-element.24.refs_3_.wide_ref, ...), custom_call_target="tpu_custom_call" | custom-call | tf_op jit(solution)/shard_map/solve/pallas_call | solution.py:444
  76.1 11.6 %all_to_all.33 = f32[32,1,1536]{2,1,0:T(1,128)S(1)} all-to-all(f32[32,1,1536]{2,1,0:T(1,128)S(1)} %bitcast.85), channel_id=1, replica_groups=mesh['sweep'=32,'grp'=4] {'sweep'}, dimensions={0} | all-to-all | bytes 393216 | tf_op jit(solution)/shard_map/all_to_all | solution.py:458
  87.7 0.7 chain.3
  88.5 11.9 %all_to_all.34 = f32[32,1,1536]{2,1,0:T(1,128)S(1)} all-to-all(f32[32,1,1536]{2,1,0:T(1,128)S(1)} %bitcast.81), channel_id=1, replica_groups=mesh['sweep'=32,'grp'=4] {'sweep'}, dimensions={0} | all-to-all | bytes 393216 | tf_op jit(solution)/shard_map/all_to_all | solution.py:458
  100.3 1.3 %finish.1 = (f32[6,128,128]{2,1,0:T(8,128)}, f32[6,128,128]{2,1,0:T(8,128)}) custom-call(f32[384,128]{1,0:T(8,128)S(1)} %bitcast.78, f32[4,6,32,128]{3,2,1,0:T(8,128)S(1)} %get-tuple-element.37.z_ref, f32[6,128,128]{2,1,0:T(8,128)S(1)} %get-tuple-element.34.refs_7_.state_ref, f32[4,108,128]{2,1,0:T(8,128)S(1)} %get-tuple-element.24.refs_3_.wide_ref, ...), custom_call_target="tpu_custom_call" | custom-call | tf_op jit(solution)/shard_map/finish/pallas_call | solution.py:444
Async XLA Ops:
  5.0 21.4 %all-to-all-start = ((f32[128,1,256]{2,1,0:T(1,128)}), f32[128,1,256]{2,1,0:T(1,128)S(1)}, u32[]{:S(2)}, u32[]{:S(2)}) async-start(f32[128,1,256]{2,1,0:T(1,128)} %bitcast.9), calls=%async_computation | async-start | bytes 262144 | tf_op jit(solution)/shard_map/all_to_all | solution.py:458

commit v5 on v4

--- a/solution.py
+++ b/solution.py
@@ -23,7 +23,6 @@
 DIAG, DOWN, RISE = 0, 1, 2
 FULL = 20
 BARE = 12
-VMEM = pl.BlockSpec(memory_space=pltpu.VMEM)
 PARAMS = pltpu.CompilerParams(vmem_limit_bytes=24 * 1024 * 1024)
 BESIDE = pl.CostEstimate(flops=20_000_000_000, bytes_accessed=4_000_000, transcendentals=0)
 
@@ -286,13 +285,14 @@
     chunk_ref, z_ref, resid_s, high_s, low_s, total_s, visc_s, forcing_s, sems = refs
     copies = fetch(((visc_hbm, visc_s), (forcing_hbm, forcing_s)), sems)
     order = order_of(order_ref)
+    if full:
+        maps = maps_ref[...]
+        for r in range(FULL - BARE):
+            chunk_ref[pl.ds(BARE + r, TILES, stride=rows), :] = maps[r]
     scatter(got_ref, point_ref, place_ref, resid_s, high_s, low_s, total_s)
     for copy in copies:
         copy.wait()
     residual(state_ref, forcing_s, visc_s, count_ref, resid_s)
-    if full:
-        for r in range(FULL - BARE):
-            chunk_ref[pl.ds(BARE + r, TILES, stride=rows), :] = maps_ref[r]
     for first in range(0, TILES, SPAN):
 
         def put(r, value):
@@ -400,7 +400,7 @@
         out_ref[pl.ds(VARS + i, TILES, stride=BARE), :] = mid_s[pl.ds(i, TILES, stride=8), :]
 
 
-def finish(back_ref, z_ref, state_ref, wide_ref, factor_ref, order_ref, new_ref, corr_ref, star_s):
+def finish(back_ref, z_ref, state_ref, wide_ref, factor_ref, order_ref, new_ref, corr_ref, star_s, ready=None):
     order = order_of(order_ref)
     for first in range(0, TILES, SPAN):
         here = slice(first, first + SPAN)
@@ -420,6 +420,25 @@
                 if corr_ref is not None:
                     corr_ref[i, places, :] = corr[i]
                 new_ref[i, places, :] = state_ref[i, places, :] + corr[i]
+        if ready is not None:
+            ready(first)
+
+
+def last_kernel(
+    back_ref, z_ref, state_ref, wide_ref, factor_ref, order_ref, new_hbm, corr_hbm, star_s, new_s, corr_s, sems
+):
+    copies = []
+
+    def ready(first):
+        rows = pl.ds(first * BLK, SPAN * BLK)
+        for src, dst in ((new_s, new_hbm), (corr_s, corr_hbm)):
+            copy = pltpu.make_async_copy(src.at[:, rows, :], dst.at[:, rows, :], sems.at[len(copies)])
+            copy.start()
+            copies.append(copy)
+
+    finish(back_ref, z_ref, state_ref, wide_ref, factor_ref, order_ref, new_s, corr_s, star_s, ready)
+    for copy in copies:
+        copy.wait()
 
 
 def middle_kernel(
@@ -439,13 +458,13 @@
     return pltpu.VMEM(dims, dtype)
 
 
-def call(kernel, name, outs, operands, scratch=(), outside=(), beside=False):
+def call(kernel, name, outs, operands, scratch=(), outside=(), beside=False, out_space=pltpu.VMEM):
     spaces = [pltpu.HBM if n in outside else pltpu.VMEM for n in range(len(operands))]
     return pl.pallas_call(
         kernel,
         out_shape=outs,
         in_specs=[pl.BlockSpec(memory_space=space) for space in spaces],
-        out_specs=[VMEM] * len(outs),
+        out_specs=[pl.BlockSpec(memory_space=out_space)] * len(outs),
         scratch_shapes=list(scratch),
         compiler_params=PARAMS,
         cost_estimate=BESIDE if beside else None,
@@ -556,7 +575,12 @@
     )
     back = exchange(entering, "sweep", TILES)
     state, correction = call(
-        finish, "finish", [jax.ShapeDtypeStruct(big, F32)] * 2, (back, z, state, wide, factors, block_order), star_scratch
+        last_kernel,
+        "last",
+        [jax.ShapeDtypeStruct(big, F32)] * 2,
+        (back, z, state, wide, factors, block_order),
+        star_scratch + [pltpu.VMEM(big, F32), pltpu.VMEM(big, F32), dma((2 * TILES // SPAN,))],
+        out_space=pltpu.HBM,
     )
     return from_rows(state)[None], from_rows(correction)[None]
 

time: 102 us -> 102 us (level)
  no operation moved by 1% of the time
where the time goes in v5:
time: 102 us; the launch traced here: 101 us
  blocking collectives  62.7 us (61%)
  Pallas kernels  18.6 us (18%)
  starting transfers between devices  11.5 us (11%)
  waiting for transfers between devices  7.63 us (7%)
    all_to_all x5, blocking collectives, exchange(): lax.all_to_all(parts, axes, split_axis=0, concat_axis=0, tiled=True)  62.7 us
    pallas_call x8, Pallas kernels, call(): pl.pallas_call(kernel, out_shape=outs, in_specs=[pl.BlockSpec(memory_spac...  18.6 us
    all_to_all x1, starting transfers between devices, exchange(): lax.all_to_all(parts, axes, split_axis=0, concat_axis=0, tiled=True)  11.5 us
    all_to_all x1, waiting for transfers between devices, exchange(): lax.all_to_all(parts, axes, split_axis=0, concat_axis=0, tiled=True)  7.63 us
  transfers between devices with their start and end apart: 1, of which 1 were waited for; matrix products, arithmetic and copies ran while one was open for 0% of the time, Pallas kernels for 2%

profile of v5, /device:TPU:1, one launch (start us, length us, event | category | flops | bytes accessed | tf_op | source)
XLA Modules:
  0.0 101.2 jit_solution(5580397789045582551)
XLA Ops:
  0.6 4.3 %first.1 = (f32[256,128]{1,0:T(8,128)}, f32[6,128,128]{2,1,0:T(8,128)S(1)}) custom-call(s32[32,128]{1,0:T(8,128)} %bitcast.95, s32[32,128]{1,0:T(8,128)} %bitcast.97, f32[6,128,128]{2,1,0:T(8,128)} %bitcast.90, f32[32,4,128]{2,1,0:T(4,128)} %bitcast.93), custom_call_target="tpu_custom_call" | custom-call | tf_op jit(solution)/shard_map/first/pallas_call | solution.py:463
  5.0 11.5 %all-to-all-start = ((f32[128,1,256]{2,1,0:T(1,128)}), f32[128,1,256]{2,1,0:T(1,128)S(1)}, u32[]{:S(2)}, u32[]{:S(2)}) async-start(f32[128,1,256]{2,1,0:T(1,128)} %bitcast.9), calls=%async_computation | async-start | bytes 262144 | tf_op jit(solution)/shard_map/all_to_all | solution.py:477
  16.5 2.2 %base.1 = (bf16[256,4096]{1,0:T(8,128)(2,1)S(1)}, f32[128,128]{1,0:T(8,128)S(1)}, f32[4,108,128]{2,1,0:T(8,128)S(1)}, f32[12,32,128]{2,1,0:T(8,128)S(1)}, f32[8,...) custom-call(s32[32,128]{1,0:T(8,128)} %bitcast.104, s32[32,128]{1,0:T(8,128)} %bitcast.105, ...), custom_call_target="tpu_custom_call" | custom-call | flops 20000000000 | bytes 4000000 | tf_op jit(solution)/shard_map/base/pallas_call | solution.py:463
  18.7 7.6 %all-to-all-done = f32[128,1,256]{2,1,0:T(1,128)S(1)} async-done(((f32[128,1,256]{2,1,0:T(1,128)}), f32[128,1,256]{2,1,0:T(1,128)S(1)}, u32[]{:S(2)}, u32[]{:S(2)}) %all-to-all-start) | async-done | bytes 131104 | tf_op jit(solution)/shard_map/all_to_all | solution.py:477
  26.3 2.7 %solve.2 = (f32[640,128]{1,0:T(8,128)S(1)}, f32[4,6,32,128]{3,2,1,0:T(8,128)S(1)}) custom-call(f32[256,128]{1,0:T(8,128)S(1)} %bitcast.82, s32[32,128]{1,0:T(8,128)S(1)} %get-tuple-element.22.refs_1_, bf16[256,4096]{1,0:T(8,128)(2,1)S(1)} %get-tuple-element.23.refs_2_, f32[4,108,128]{2,1,0:T(8,128)S(1)} %get-tuple-element.24.refs_3_.wide_ref, ...), custom_call_target="tpu_custom_call" | custom-call | tf_op jit(solution)/shard_map/solve/pallas_call | solution.py:463
  29.0 13.3 %all_to_all.30 = f32[32,1,2560]{2,1,0:T(1,128)S(1)} all-to-all(f32[32,1,2560]{2,1,0:T(1,128)S(1)} %bitcast.84), channel_id=1, replica_groups=mesh['sweep'=32,'grp'=4] {'sweep'}, dimensions={0} | all-to-all | bytes 655360 | tf_op jit(solution)/shard_map/all_to_all | solution.py:477
  42.3 1.3 %chain.2 = (f32[384,128]{1,0:T(8,128)S(1)}, f32[256,4608]{1,0:T(8,128)S(1)}) custom-call(f32[640,128]{1,0:T(8,128)S(1)} %bitcast.76), custom_call_target="tpu_custom_call" | custom-call | tf_op jit(solution)/shard_map/chain/pallas_call | solution.py:463
  43.6 11.8 %all_to_all.31 = f32[32,1,1536]{2,1,0:T(1,128)S(1)} all-to-all(f32[32,1,1536]{2,1,0:T(1,128)S(1)} %bitcast.86), channel_id=1, replica_groups=mesh['sweep'=32,'grp'=4] {'sweep'}, dimensions={0} | all-to-all | bytes 393216 | tf_op jit(solution)/shard_map/all_to_all | solution.py:477
  55.4 3.4 %middle.1 = (f32[6,128,128]{2,1,0:T(8,128)S(1)}, f32[256,128]{1,0:T(8,128)S(1)}) custom-call(f32[384,128]{1,0:T(8,128)S(1)} %bitcast.79, f32[4,6,32,128]{3,2,1,0:T(8,128)S(1)} %get-tuple-element.32.z_ref, f32[6,128,128]{2,1,0:T(8,128)S(1)} %get-tuple-element.28.refs_7_.state_ref, f32[4,108,128]{2,1,0:T(8,128)S(1)} %get-tuple-element.24.refs_3_.wide_ref, ...), custom_call_target="tpu_custom_call" | custom-call | tf_op jit(solution)/shard_map/middle/pallas_call | solution.py:463
  58.8 14.1 %all_to_all.32 = f32[128,1,256]{2,1,0:T(1,128)S(1)} all-to-all(f32[128,1,256]{2,1,0:T(1,128)S(1)} %bitcast.87), channel_id=1, replica_groups=mesh['sweep'=32,'grp'=4] {'sweep','grp'}, dimensions={0} | all-to-all | bytes 262144 | tf_op jit(solution)/shard_map/all_to_all | solution.py:477
  72.9 2.7 %solve.3 = (f32[384,128]{1,0:T(8,128)S(1)}, f32[4,6,32,128]{3,2,1,0:T(8,128)S(1)}) custom-call(f32[256,128]{1,0:T(8,128)S(1)} %bitcast.83, s32[32,128]{1,0:T(8,128)S(1)} %get-tuple-element.22.refs_1_, bf16[256,4096]{1,0:T(8,128)(2,1)S(1)} %get-tuple-element.23.refs_2_, f32[4,108,128]{2,1,0:T(8,128)S(1)} %get-tuple-element.24.refs_3_.wide_ref, ...), custom_call_target="tpu_custom_call" | custom-call | tf_op jit(solution)/shard_map/solve/pallas_call | solution.py:463
  75.6 11.6 %all_to_all.33 = f32[32,1,1536]{2,1,0:T(1,128)S(1)} all-to-all(f32[32,1,1536]{2,1,0:T(1,128)S(1)} %bitcast.85), channel_id=1, replica_groups=mesh['sweep'=32,'grp'=4] {'sweep'}, dimensions={0} | all-to-all | bytes 393216 | tf_op jit(solution)/shard_map/all_to_all | solution.py:477
  87.3 0.7 chain.3
  88.0 11.9 %all_to_all.34 = f32[32,1,1536]{2,1,0:T(1,128)S(1)} all-to-all(f32[32,1,1536]{2,1,0:T(1,128)S(1)} %bitcast.81), channel_id=1, replica_groups=mesh['sweep'=32,'grp'=4] {'sweep'}, dimensions={0} | all-to-all | bytes 393216 | tf_op jit(solution)/shard_map/all_to_all | solution.py:477
  99.9 1.2 %last.1 = (f32[6,128,128]{2,1,0:T(8,128)}, f32[6,128,128]{2,1,0:T(8,128)}) custom-call(f32[384,128]{1,0:T(8,128)S(1)} %bitcast.78, f32[4,6,32,128]{3,2,1,0:T(8,128)S(1)} %get-tuple-element.37.z_ref, f32[6,128,128]{2,1,0:T(8,128)S(1)} %get-tuple-element.34.refs_7_.state_ref, f32[4,108,128]{2,1,0:T(8,128)S(1)} %get-tuple-element.24.refs_3_.wide_ref, ...), custom_call_target="tpu_custom_call" | custom-call | tf_op jit(solution)/shard_map/last/pallas_call | solution.py:463
Async XLA Ops:
  5.0 21.4 %all-to-all-start = ((f32[128,1,256]{2,1,0:T(1,128)}), f32[128,1,256]{2,1,0:T(1,128)S(1)}, u32[]{:S(2)}, u32[]{:S(2)}) async-start(f32[128,1,256]{2,1,0:T(1,128)} %bitcast.9), calls=%async_computation | async-start | bytes 262144 | tf_op jit(solution)/shard_map/all_to_all | solution.py:477

commit v6 on v5

--- a/solution.py
+++ b/solution.py
@@ -534,7 +534,7 @@
             pltpu.VMEM((HALF, SLOTS * LANES), BF16),
             pltpu.VMEM((3, VARS, BLK, VARS), F32),
             pltpu.VMEM((3 * BLK, VARS, VARS), F32),
-            pltpu.VMEM((3 * SQUARE * BLK, LANES), F32),
+            pltpu.VMEM((3 * SQUARE * BLK + 8 * BLK, LANES), F32),
             pltpu.VMEM((8, LANES), F32),
             dma((9,)),
         ],

time: 102 us -> 102 us (level)
  no operation moved by 1% of the time
where the time goes in v6:
time: 102 us; the launch traced here: 101 us
  blocking collectives  62.7 us (61%)
  Pallas kernels  18.6 us (18%)
  starting transfers between devices  11.5 us (11%)
  waiting for transfers between devices  7.63 us (7%)
    all_to_all x5, blocking collectives, exchange(): lax.all_to_all(parts, axes, split_axis=0, concat_axis=0, tiled=True)  62.7 us
    pallas_call x8, Pallas kernels, call(): pl.pallas_call(kernel, out_shape=outs, in_specs=[pl.BlockSpec(memory_spac...  18.6 us
    all_to_all x1, starting transfers between devices, exchange(): lax.all_to_all(parts, axes, split_axis=0, concat_axis=0, tiled=True)  11.5 us
    all_to_all x1, waiting for transfers between devices, exchange(): lax.all_to_all(parts, axes, split_axis=0, concat_axis=0, tiled=True)  7.63 us
  transfers between devices with their start and end apart: 1, of which 1 were waited for; matrix products, arithmetic and copies ran while one was open for 0% of the time, Pallas kernels for 2%

profile of v6, /device:TPU:1, one launch (start us, length us, event | category | flops | bytes accessed | tf_op | source)
XLA Modules:
  0.0 101.2 jit_solution(14739816349482137137)
XLA Ops:
  0.6 4.3 %first.1 = (f32[256,128]{1,0:T(8,128)}, f32[6,128,128]{2,1,0:T(8,128)S(1)}) custom-call(s32[32,128]{1,0:T(8,128)} %bitcast.95, s32[32,128]{1,0:T(8,128)} %bitcast.97, f32[6,128,128]{2,1,0:T(8,128)} %bitcast.90, f32[32,4,128]{2,1,0:T(4,128)} %bitcast.93), custom_call_target="tpu_custom_call" | custom-call | tf_op jit(solution)/shard_map/first/pallas_call | solution.py:463
  5.0 11.5 %all-to-all-start = ((f32[128,1,256]{2,1,0:T(1,128)}), f32[128,1,256]{2,1,0:T(1,128)S(1)}, u32[]{:S(2)}, u32[]{:S(2)}) async-start(f32[128,1,256]{2,1,0:T(1,128)} %bitcast.9), calls=%async_computation | async-start | bytes 262144 | tf_op jit(solution)/shard_map/all_to_all | solution.py:477
  16.5 2.2 %base.1 = (bf16[256,4096]{1,0:T(8,128)(2,1)S(1)}, f32[128,128]{1,0:T(8,128)S(1)}, f32[4,108,128]{2,1,0:T(8,128)S(1)}, f32[12,32,128]{2,1,0:T(8,128)S(1)}, f32[8,...) custom-call(s32[32,128]{1,0:T(8,128)} %bitcast.104, s32[32,128]{1,0:T(8,128)} %bitcast.105, ...), custom_call_target="tpu_custom_call" | custom-call | flops 20000000000 | bytes 4000000 | tf_op jit(solution)/shard_map/base/pallas_call | solution.py:463
  18.7 7.6 %all-to-all-done = f32[128,1,256]{2,1,0:T(1,128)S(1)} async-done(((f32[128,1,256]{2,1,0:T(1,128)}), f32[128,1,256]{2,1,0:T(1,128)S(1)}, u32[]{:S(2)}, u32[]{:S(2)}) %all-to-all-start) | async-done | bytes 131104 | tf_op jit(solution)/shard_map/all_to_all | solution.py:477
  26.3 2.7 %solve.2 = (f32[640,128]{1,0:T(8,128)S(1)}, f32[4,6,32,128]{3,2,1,0:T(8,128)S(1)}) custom-call(f32[256,128]{1,0:T(8,128)S(1)} %bitcast.82, s32[32,128]{1,0:T(8,128)S(1)} %get-tuple-element.22.refs_1_, bf16[256,4096]{1,0:T(8,128)(2,1)S(1)} %get-tuple-element.23.refs_2_, f32[4,108,128]{2,1,0:T(8,128)S(1)} %get-tuple-element.24.refs_3_.wide_ref, ...), custom_call_target="tpu_custom_call" | custom-call | tf_op jit(solution)/shard_map/solve/pallas_call | solution.py:463
  29.0 13.3 %all_to_all.30 = f32[32,1,2560]{2,1,0:T(1,128)S(1)} all-to-all(f32[32,1,2560]{2,1,0:T(1,128)S(1)} %bitcast.84), channel_id=1, replica_groups=mesh['sweep'=32,'grp'=4] {'sweep'}, dimensions={0} | all-to-all | bytes 655360 | tf_op jit(solution)/shard_map/all_to_all | solution.py:477
  42.3 1.4 %chain.2 = (f32[384,128]{1,0:T(8,128)S(1)}, f32[256,4608]{1,0:T(8,128)S(1)}) custom-call(f32[640,128]{1,0:T(8,128)S(1)} %bitcast.76), custom_call_target="tpu_custom_call" | custom-call | tf_op jit(solution)/shard_map/chain/pallas_call | solution.py:463
  43.6 11.8 %all_to_all.31 = f32[32,1,1536]{2,1,0:T(1,128)S(1)} all-to-all(f32[32,1,1536]{2,1,0:T(1,128)S(1)} %bitcast.86), channel_id=1, replica_groups=mesh['sweep'=32,'grp'=4] {'sweep'}, dimensions={0} | all-to-all | bytes 393216 | tf_op jit(solution)/shard_map/all_to_all | solution.py:477
  55.4 3.4 %middle.1 = (f32[6,128,128]{2,1,0:T(8,128)S(1)}, f32[256,128]{1,0:T(8,128)S(1)}) custom-call(f32[384,128]{1,0:T(8,128)S(1)} %bitcast.79, f32[4,6,32,128]{3,2,1,0:T(8,128)S(1)} %get-tuple-element.32.z_ref, f32[6,128,128]{2,1,0:T(8,128)S(1)} %get-tuple-element.28.refs_7_.state_ref, f32[4,108,128]{2,1,0:T(8,128)S(1)} %get-tuple-element.24.refs_3_.wide_ref, ...), custom_call_target="tpu_custom_call" | custom-call | tf_op jit(solution)/shard_map/middle/pallas_call | solution.py:463
  58.8 14.1 %all_to_all.32 = f32[128,1,256]{2,1,0:T(1,128)S(1)} all-to-all(f32[128,1,256]{2,1,0:T(1,128)S(1)} %bitcast.87), channel_id=1, replica_groups=mesh['sweep'=32,'grp'=4] {'sweep','grp'}, dimensions={0} | all-to-all | bytes 262144 | tf_op jit(solution)/shard_map/all_to_all | solution.py:477
  72.9 2.7 %solve.3 = (f32[384,128]{1,0:T(8,128)S(1)}, f32[4,6,32,128]{3,2,1,0:T(8,128)S(1)}) custom-call(f32[256,128]{1,0:T(8,128)S(1)} %bitcast.83, s32[32,128]{1,0:T(8,128)S(1)} %get-tuple-element.22.refs_1_, bf16[256,4096]{1,0:T(8,128)(2,1)S(1)} %get-tuple-element.23.refs_2_, f32[4,108,128]{2,1,0:T(8,128)S(1)} %get-tuple-element.24.refs_3_.wide_ref, ...), custom_call_target="tpu_custom_call" | custom-call | tf_op jit(solution)/shard_map/solve/pallas_call | solution.py:463
  75.6 11.6 %all_to_all.33 = f32[32,1,1536]{2,1,0:T(1,128)S(1)} all-to-all(f32[32,1,1536]{2,1,0:T(1,128)S(1)} %bitcast.85), channel_id=1, replica_groups=mesh['sweep'=32,'grp'=4] {'sweep'}, dimensions={0} | all-to-all | bytes 393216 | tf_op jit(solution)/shard_map/all_to_all | solution.py:477
  87.3 0.7 chain.3
  88.0 11.9 %all_to_all.34 = f32[32,1,1536]{2,1,0:T(1,128)S(1)} all-to-all(f32[32,1,1536]{2,1,0:T(1,128)S(1)} %bitcast.81), channel_id=1, replica_groups=mesh['sweep'=32,'grp'=4] {'sweep'}, dimensions={0} | all-to-all | bytes 393216 | tf_op jit(solution)/shard_map/all_to_all | solution.py:477
  99.9 1.2 %last.1 = (f32[6,128,128]{2,1,0:T(8,128)}, f32[6,128,128]{2,1,0:T(8,128)}) custom-call(f32[384,128]{1,0:T(8,128)S(1)} %bitcast.78, f32[4,6,32,128]{3,2,1,0:T(8,128)S(1)} %get-tuple-element.37.z_ref, f32[6,128,128]{2,1,0:T(8,128)S(1)} %get-tuple-element.34.refs_7_.state_ref, f32[4,108,128]{2,1,0:T(8,128)S(1)} %get-tuple-element.24.refs_3_.wide_ref, ...), custom_call_target="tpu_custom_call" | custom-call | tf_op jit(solution)/shard_map/last/pallas_call | solution.py:463
Async XLA Ops:
  5.0 21.4 %all-to-all-start = ((f32[128,1,256]{2,1,0:T(1,128)}), f32[128,1,256]{2,1,0:T(1,128)S(1)}, u32[]{:S(2)}, u32[]{:S(2)}) async-start(f32[128,1,256]{2,1,0:T(1,128)} %bitcast.9), calls=%async_computation | async-start | bytes 262144 | tf_op jit(solution)/shard_map/all_to_all | solution.py:477
